TPU v7x, 128 devices: a whole 4x4x4 slice. The times are simulated.
128 devices in a mesh: pair: 8 (over z, y_lo), tile: 16 (over y_hi, x, core).
Axes of the slice: x: 4, y: 4 (y_hi: 2, y_lo: 2; y = y_hi * 2 + y_lo), z: 4, core: 2. Of those that a mesh axis runs over, the one named last changes fastest.
Arguments:
- phases: bfloat16 [1536, 131072], P(('pair', 'tile')), may hold values from -5 to 5
- pair_dates: int32 [1536, 2], replicated, may hold values from 0 to 303, as said below
- weights: float32 [2, 1536], replicated, may hold values from 0.25 to 4
- coords: int32 [2, 131072], P(None, ('pair', 'tile')), may hold values from 0 to 4095, as said below
Outputs:
- coefficients: float32 [32, 131072], P(None, ('pair', 'tile'))
- screens: float32 [304, 256], P('pair')
Inputs may be any that keep to these rules, and one draw needn't show every extreme that they name: `pair_dates`: in every row the first date is earlier than the second, at most 15 dates before it. `coords`: pixel b * 1024 + j with j < 512 has its row among the 512 rows of band b // 16 and its column among the 256 columns of band b % 16; the other pixels lie anywhere in the frame.
All inputs are finite; a program needn't handle non-finite values.
Results may differ from a plain program's by a relative error of at most 0.006.
Values may be sent and summed in bfloat16 or wider, within the bound.
A program may use at most 128 MiB of HBM per device.

v0:
```python
import jax
import jax.numpy as jnp
from jax import lax
from jax.sharding import PartitionSpec as P

DATES = 304
NB = 32
KNOTS = 16
FRAME = 4096
ITERS = 2
SCREEN = 256
PB = 256


fit_ridge = 0.5
date_ridge = 1.0
knot_ridge = 1.0


def spline_rows(positions, basis_count):
    centers = jnp.arange(basis_count).astype(jnp.float32) - 1.0
    offset = jnp.abs(positions[None, :] - centers[:, None])
    near_part = 2.0 / 3.0 - offset * offset + 0.5 * offset * offset * offset
    remain = jnp.maximum(2.0 - offset, 0.0)
    return jnp.where(offset < 1.0, near_part, remain * remain * remain / 6.0)


def pair_setup(pair_dates, weights):
    date_axis = jnp.arange(DATES).astype(jnp.float32) * ((NB - 3.0) / (DATES - 1.0))
    temporal = spline_rows(date_axis, NB).T
    columns = jnp.arange(DATES)
    incidence = (columns[None, :] == pair_dates[:, 1:2]).astype(jnp.float32) - (
        columns[None, :] == pair_dates[:, 0:1]
    ).astype(jnp.float32)
    design = jnp.dot(incidence, temporal, precision=lax.Precision.HIGHEST)
    fit_solves = []
    date_solves = []
    for iteration in range(ITERS):
        weight = weights[iteration]
        scaled = design * weight[:, None]
        normal = jnp.dot(design.T, scaled, precision=lax.Precision.HIGHEST) + fit_ridge * jnp.eye(
            NB, dtype=jnp.float32
        )
        factor = jnp.linalg.cholesky(normal)
        fit_solves.append(jax.scipy.linalg.cho_solve((factor, True), scaled.T).astype(jnp.bfloat16))
        weighted = incidence * weight[:, None]
        date_normal = jnp.dot(
            incidence.T, weighted, precision=lax.Precision.HIGHEST
        ) + date_ridge * jnp.eye(DATES, dtype=jnp.float32)
        date_factor = jnp.linalg.cholesky(date_normal)
        date_solves.append(
            jax.scipy.linalg.cho_solve((date_factor, True), weighted.T).astype(jnp.bfloat16)
        )
    return (design, fit_solves, date_solves)


def knot_basis(coords):
    scaled = coords.astype(jnp.float32) * ((KNOTS - 3.0) / FRAME)
    row_part = spline_rows(scaled[0], KNOTS)
    col_part = spline_rows(scaled[1], KNOTS)
    return (row_part[:, None, :] * col_part[None, :, :]).reshape(KNOTS * KNOTS, -1)


def fit_pass(corrected, fit_solve, date_solve, design):
    coeffs = jnp.dot(fit_solve, corrected, preferred_element_type=jnp.float32)
    fitted = jnp.dot(design, coeffs, precision=lax.Precision.HIGHEST)
    residual = (corrected.astype(jnp.float32) - fitted).astype(jnp.bfloat16)
    date_field = jnp.dot(date_solve, residual, preferred_element_type=jnp.float32).astype(
        jnp.bfloat16
    )
    return (coeffs, date_field)


def local(phases, pair_dates, weights, coords):
    pair_count = lax.axis_size("pair")
    tile_count = lax.axis_size("tile")
    devices = pair_count * tile_count
    local_pairs = phases.shape[0]
    pair_total = local_pairs * devices
    pixels = coords.shape[1]
    groups = pixels // PB
    design, fit_solves, date_solves = pair_setup(pair_dates, weights)
    knot_f32 = knot_basis(coords)
    gram_part = jnp.dot(knot_f32, knot_f32.T, precision=lax.Precision.HIGHEST)
    gram_total = lax.psum(gram_part, ("pair", "tile")) + knot_ridge * jnp.eye(
        SCREEN, dtype=jnp.float32
    )
    factor = jnp.linalg.cholesky(gram_total)
    knot_rows = knot_f32.astype(jnp.bfloat16)
    date_share = DATES // pair_count
    first_date = lax.axis_index("pair") * date_share
    shaped = phases.reshape(local_pairs, devices, groups, PB)
    pixel_block = lax.all_to_all(shaped, ("pair", "tile"), split_axis=1, concat_axis=0, tiled=True)
    item_count = pixel_block.shape[2]
    stacked = pixel_block.reshape(pair_total, item_count * PB)
    coeffs, date_field = fit_pass(stacked, fit_solves[0], date_solves[0], design)
    arrived, date_field = (
        stacked.reshape(pair_total, item_count, PB),
        date_field.reshape(DATES, item_count, PB),
    )
    arrived = arrived.reshape(pair_total, pixels)
    date_field = date_field.reshape(DATES, pixels)
    screens = jnp.zeros((DATES, SCREEN), jnp.float32)
    own_screens = lax.dynamic_slice_in_dim(screens, first_date, date_share, 0)
    coeffs = None
    for iteration in range(ITERS):
        if iteration > 0:
            screen_field = jnp.dot(
                screens.astype(jnp.bfloat16), knot_rows, preferred_element_type=jnp.float32
            )
            shifts = jnp.take(screen_field, pair_dates[:, 1], axis=0) - jnp.take(
                screen_field, pair_dates[:, 0], axis=0
            )
            corrected = (arrived.astype(jnp.float32) - shifts).astype(jnp.bfloat16)
            coeffs, date_field = fit_pass(
                corrected, fit_solves[iteration], date_solves[iteration], design
            )
        partial_value = lax.dot_general(
            date_field, knot_rows, (((1,), (1,)), ((), ())), preferred_element_type=jnp.float32
        )
        totals = lax.psum(partial_value, ("pair", "tile"))
        change = jax.scipy.linalg.cho_solve((factor, True), totals.T).T
        screens = screens + change
        own_screens = lax.dynamic_slice_in_dim(screens, first_date, date_share, 0)
    return (coeffs, own_screens)


def solution(mesh):
    return jax.shard_map(
        local,
        mesh=mesh,
        in_specs=(P(("pair", "tile"), None), P(), P(), P(None, ("pair", "tile"))),
        out_specs=(P(None, ("pair", "tile")), P("pair", None)),
        check_vma=False,
    )
```

profile of v0, /device:TPU:1, one launch (start us, length us, event | category | flops | bytes accessed | tf_op | source)
XLA Modules:
  0.0 697.0 jit_solution(12757352463045270878)
XLA Ops:
  7.2 6.5 reshape.195
  16.5 11.9 %all-to-all-start = ((bf16[12,128,4,256]{3,2,0,1:T(4,128)(2,1)}), bf16[12,128,4,256]{3,2,0,1:T(4,128)(2,1)}, u32[]{:S(2)}, u32[]{:S(2)}) async-start(bf16[12,128,4,256]{3,2,0,1:T(4,128)(2,1)} %copy.8), calls=%async_computation | async-start | bytes 6291456 | tf_op jit(solution)/shard_map/all_to_all | solution.py:93
  29.6 5.6 fusion.15
  35.2 6.4 fusion.18
  49.2 11.7 %cholesky.385 = f32[128,128]{1,0:T(8,128)S(1)} custom-call(f32[128,128]{1,0:T(8,128)S(1)} %cholesky.509), custom_call_target="Cholesky" | custom-call | tf_op jit(solution)/shard_map/jit(cholesky)/cholesky | solution.py:50
  60.9 9.8 %custom-call.49 = f32[1,128,128]{1,2,0:T(8,128)S(1)} custom-call(f32[1,128,128]{2,1,0:T(8,128)S(1)} %get-tuple-element.93), custom_call_target="InvertDiagBlocksLowerTriangular" | custom-call | tf_op jit(solution)/shard_map/jit(cholesky)/cholesky | solution.py:50
  73.1 12.1 %cholesky.404 = f32[128,128]{1,0:T(8,128)S(1)} custom-call(f32[128,128]{1,0:T(8,128)S(1)} %cholesky.513), custom_call_target="Cholesky" | custom-call | tf_op jit(solution)/shard_map/jit(cholesky)/cholesky | solution.py:50
  85.2 9.8 %custom-call.50 = f32[1,128,128]{1,2,0:T(8,128)S(1)} custom-call(f32[1,128,128]{2,1,0:T(8,128)S(1)} %get-tuple-element.90), custom_call_target="InvertDiagBlocksLowerTriangular" | custom-call | tf_op jit(solution)/shard_map/jit(cholesky)/cholesky | solution.py:50
  96.2 4.4 cholesky.426
  106.9 11.7 %cholesky.453 = f32[128,128]{1,0:T(8,128)S(1)} custom-call(f32[128,128]{1,0:T(8,128)S(1)} %cholesky.517), custom_call_target="Cholesky" | custom-call | tf_op jit(solution)/shard_map/jit(cholesky)/cholesky | solution.py:50
  118.6 9.8 %custom-call.54 = f32[1,128,128]{1,2,0:T(8,128)S(1)} custom-call(f32[1,128,128]{2,1,0:T(8,128)S(1)} %get-tuple-element.84), custom_call_target="InvertDiagBlocksLowerTriangular" | custom-call | tf_op jit(solution)/shard_map/jit(cholesky)/cholesky | solution.py:50
  130.8 11.9 %cholesky.472 = f32[128,128]{1,0:T(8,128)S(1)} custom-call(f32[128,128]{1,0:T(8,128)S(1)} %cholesky.521), custom_call_target="Cholesky" | custom-call | tf_op jit(solution)/shard_map/jit(cholesky)/cholesky | solution.py:50
  142.7 9.8 %custom-call.55 = f32[1,128,128]{1,2,0:T(8,128)S(1)} custom-call(f32[1,128,128]{2,1,0:T(8,128)S(1)} %get-tuple-element.81), custom_call_target="InvertDiagBlocksLowerTriangular" | custom-call | tf_op jit(solution)/shard_map/jit(cholesky)/cholesky | solution.py:50
  153.6 4.4 cholesky.494
  162.3 4.0 while.10
  167.8 30.3 %custom-call.56 = f32[3,128,128]{1,2,0:T(8,128)S(1)} custom-call(f32[3,128,128]{2,1,0:T(8,128)} %pad_maximum_fusion.2), custom_call_target="InvertDiagBlocksLowerTriangular" | custom-call | tf_op jit(solution)/shard_map/jit(_cho_solve)/triangular_solve | solution.py:52
  204.3 5.2 while.8
  210.4 29.9 %custom-call.51 = f32[3,128,128]{1,2,0:T(8,128)S(1)} custom-call(f32[3,128,128]{2,1,0:T(8,128)S(1)} %pad_maximum_fusion.1), custom_call_target="InvertDiagBlocksLowerTriangular" | custom-call | tf_op jit(solution)/shard_map/jit(_cho_solve)/triangular_solve | solution.py:52
  292.3 5.5 fusion
  297.8 3.6 fusion.29
  304.3 144.7 %all-reduce.10.cloned.1.call-done = (f32[256,304]{0,1:T(8,128)}, f32[256,256]{0,1:T(8,128)}) async-done(((f32[256,304]{0,1:T(8,128)}, f32[256,256]{0,1:T(8,128)}), (f32[256,304]{0,1:T(8,128)}, f32[256,256]{0,1:T(8,128)})) %all-reduce.10.cloned.1.call-update) | async-done | bytes 573456 | tf_op jit(solution)/shard_map/psum | solution.py:121
  451.2 11.7 %cholesky.149 = f32[128,128]{1,0:T(8,128)S(1)} custom-call(f32[128,128]{1,0:T(8,128)S(1)} %cholesky.506), custom_call_target="Cholesky" | custom-call | tf_op jit(solution)/shard_map/jit(cholesky)/cholesky | solution.py:88
  462.9 9.8 %custom-call.42 = f32[1,128,128]{1,2,0:T(8,128)S(1)} custom-call(f32[1,128,128]{2,1,0:T(8,128)S(1)} %get-tuple-element.88), custom_call_target="InvertDiagBlocksLowerTriangular" | custom-call | tf_op jit(solution)/shard_map/jit(cholesky)/cholesky | solution.py:88
  473.2 11.7 %cholesky.170 = f32[128,128]{1,0:T(8,128)S(1)} custom-call(f32[128,128]{1,0:T(8,128)S(1)} %convolution_subtract_fusion.14), custom_call_target="Cholesky" | custom-call | tf_op jit(solution)/shard_map/jit(cholesky)/cholesky | solution.py:88
  487.5 4.2 while.9
  491.8 19.7 %custom-call.53 = f32[2,128,128]{1,2,0:T(8,128)S(1)} custom-call(f32[2,128,128]{2,1,0:T(8,128)S(1)} %get-tuple-element.37), custom_call_target="InvertDiagBlocksLowerTriangular" | custom-call | tf_op jit(solution)/shard_map/jit(_cho_solve)/triangular_solve | solution.py:122
  514.0 5.8 gather_fusion
  519.8 5.8 gather_fusion.1
  525.7 6.4 fusion.1
  533.4 5.6 subtract_convert_fusion
  539.0 3.6 fusion.30
  542.6 141.8 %all-reduce.8.cloned.1.call-done = f32[256,304]{0,1:T(8,128)} async-done(((f32[256,304]{0,1:T(8,128)}), f32[256,304]{0,1:T(8,128)}) %all-reduce.8.cloned.1.call-update) | async-done | bytes 311312 | tf_op jit(solution)/shard_map/psum | solution.py:121
  (217 shorter events, 114.6 us)
Async XLA Ops:
  16.5 13.0 %copy-start.26 = (s32[1536,2]{0,1:T(2,128)S(1)}, s32[1536,2]{0,1:T(2,128)}, u32[]{:S(2)}) copy-start(s32[1536,2]{0,1:T(2,128)} %param.15) | copy-start | bytes 36868
  16.5 13.1 %copy-start.27 = (f32[2,1536]{1,0:T(2,128)S(1)}, f32[2,1536]{1,0:T(2,128)}, u32[]{:S(2)}) copy-start(f32[2,1536]{1,0:T(2,128)} %param.16) | copy-start | bytes 36868
  16.5 272.5 %all-to-all-start = ((bf16[12,128,4,256]{3,2,0,1:T(4,128)(2,1)}), bf16[12,128,4,256]{3,2,0,1:T(4,128)(2,1)}, u32[]{:S(2)}, u32[]{:S(2)}) async-start(bf16[12,128,4,256]{3,2,0,1:T(4,128)(2,1)} %copy.8), calls=%async_computation | async-start | bytes 6291456 | tf_op jit(solution)/shard_map/all_to_all | solution.py:93
  28.4 420.6 %all-reduce.10.cloned.1.call-start = ((), (), s32[]{:S(2)}) async-start(), calls=%async_computation.2 | async-start | bytes 1146880 | tf_op jit(solution)/shard_map/psum | solution.py:121
  29.6 17.9 %copy-start.23 = (f32[1536]{0:T(1024)}, f32[1536]{0:T(1024)S(1)}, u32[]{:S(2)}) copy-start(f32[1536]{0:T(1024)S(1)} %get-tuple-element.40) | copy-start | bytes 18436
  105.0 57.3 %copy-start.32 = (s32[2]{0:T(128)S(1)}, s32[2]{0:T(128)}, u32[]{:S(2)}) copy-start(s32[2]{0:T(128)} %iota_multiply_fusion) | copy-start | bytes 28
  158.0 3.1 copy-start.12
  166.4 31.8 %copy-start.8 = (f32[304,304]{1,0:T(8,128)}, f32[304,304]{1,0:T(8,128)S(1)}, u32[]{:S(2)}) copy-start(f32[304,304]{1,0:T(8,128)S(1)} %get-tuple-element.259) | copy-start | bytes 1108996
  166.4 31.8 %copy-start.30 = (s32[2,2]{1,0:T(2,128)}, s32[2,2]{1,0:T(2,128)S(1)}, u32[]{:S(2)}) copy-start(s32[2,2]{1,0:T(2,128)S(1)} %get-tuple-element.269) | copy-start | bytes 52
  201.5 1.9 copy-start.1
  204.2 79.1 %copy-start.6 = (f32[48,1536]{1,0:T(8,128)}, f32[48,1536]{1,0:T(8,128)S(1)}, u32[]{:S(2)}) copy-start(f32[48,1536]{1,0:T(8,128)S(1)} %fusion.141) | copy-start | bytes 884740
  240.3 2.1 copy-start.18
  272.1 5.6 copy-start.19
  276.9 2.5 copy-start.7
  278.5 4.0 copy-start.4
  278.5 2.4 copy-start.2
  283.3 2.7 copy-start.3
  289.0 2.7 copy-start.21
  291.7 6.1 copy-start
  297.8 3.7 copy-start.24
  301.5 383.0 %all-reduce.8.cloned.1.call-start = ((), (), s32[]{:S(2)}) async-start(), calls=%async_computation.1 | async-start | bytes 622592 | tf_op jit(solution)/shard_map/psum | solution.py:121
  301.6 186.0 %copy-start.31 = (s32[2,2]{1,0:T(2,128)S(1)}, s32[2,2]{1,0:T(2,128)}, u32[]{:S(2)}) copy-start(s32[2,2]{1,0:T(2,128)} %get-tuple-element.270) | copy-start | bytes 52
  449.0 62.5 %copy-start.22 = (f32[256,304]{0,1:T(8,128)S(1)}, f32[256,304]{0,1:T(8,128)}, u32[]{:S(2)}) copy-start(f32[256,304]{0,1:T(8,128)} %get-tuple-element.68) | copy-start | bytes 933892
  472.7 40.9 %copy-start.11 = (bf16[16,16,1024]{2,1,0:T(8,128)(2,1)S(1)}, bf16[16,16,1024]{2,1,0:T(8,128)(2,1)}, u32[]{:S(2)}) copy-start(bf16[16,16,1024]{2,1,0:T(8,128)(2,1)} %get-tuple-element.77) | copy-start | bytes 1572868
  491.8 21.5 %copy-start.5 = (f32[256,256]{1,0:T(8,128)}, f32[256,256]{1,0:T(8,128)S(1)}, u32[]{:S(2)}) copy-start(f32[256,256]{1,0:T(8,128)S(1)} %get-tuple-element.257) | copy-start | bytes 786436
  511.5 2.5 copy-start.25
  513.6 6.2 copy-start.13
  519.8 5.8 copy-start.28
  519.8 5.8 copy-start.29
  525.7 6.4 copy-start.20
  539.0 145.5 %copy-start.10 = (f32[2,128,128]{1,2,0:T(8,128)S(1)}, f32[2,128,128]{1,2,0:T(8,128)}, u32[]{:S(2)}) copy-start(f32[2,128,128]{1,2,0:T(8,128)} %copy-done.9) | copy-start | bytes 393220
  542.6 146.7 %copy-start.14 = (f32[128,304]{0,1:T(8,128)S(1)}, f32[128,304]{0,1:T(8,128)}, u32[]{:S(2)}) copy-start(f32[128,304]{0,1:T(8,128)} %copy-done.13) | copy-start | bytes 466948
  (4 other events, 4.1 us)
Sparse Core Ops, SparseCore 0:
  301.6 147.3 all-reduce.9
  542.8 141.6 all-reduce.7
where the time goes:
time: 704 us; the launch traced here: 697 us
  waiting for transfers between devices  287 us (41%)
  other arithmetic  252 us (36%)
  matrix products  83.5 us (12%)
  local copies, waits for them, and re-layouts  42.3 us (6%)
  between operations  20.2 us (3%)
  starting transfers between devices  12.4 us (2%)
    psum x2, waiting for transfers between devices, local(): totals = lax.psum(partial_value, ('pair', 'tile'))  287 us
    another operation x20, other arithmetic, pair_setup(): date_factor = jnp.linalg.cholesky(date_normal)  98.1 us
    another operation x9, other arithmetic, pair_setup(): jax.scipy.linalg.cho_solve((date_factor, True), weighted.T)  63.6 us
    another operation x7, other arithmetic, local(): factor = jnp.linalg.cholesky(gram_total)  34.6 us
    another operation x20, matrix products, pair_setup(): jax.scipy.linalg.cho_solve((date_factor, True), weighted.T)  28.7 us
    another operation x3, other arithmetic, local(): change = jax.scipy.linalg.cho_solve((factor, True), totals.T).T  20.3 us
  transfers between devices with their start and end apart: 3, of which 2 were waited for; matrix products, arithmetic and copies ran while one was open for 37% of the time, Pallas kernels for 0%

commit v1 on v0

v1 whole, which is shorter than its diff:
```python
import functools

import jax
import jax.numpy as jnp
from jax import lax
from jax.experimental import pallas as pl
from jax.experimental.pallas import tpu as pltpu
from jax.sharding import PartitionSpec as P

MESH = pl.DeviceIdType.MESH
HI = lax.Precision.HIGHEST
F32, BF16 = jnp.float32, jnp.bfloat16
DATES, NB, KNOTS, FRAME, SCREEN = 304, 32, 16, 4096, 256
PAIRS, SLOTS, DEVICES, PIX = 12, 16, 128, 1024
N_TILE = 16
EVEN, ODD = 160, 144
KP = SLOTS * DEVICES
OWN = 40
VMEM_LIMIT = 60 * 1024 * 1024

def nn(a, b, precision=None):
    return lax.dot_general(a, b, (((1,), (0,)), ((), ())), precision=precision, preferred_element_type=F32)

def nt(a, b, precision=None):
    return lax.dot_general(a, b, (((1,), (1,)), ((), ())), precision=precision, preferred_element_type=F32)

def split2(x):
    hi = x.astype(BF16)
    return hi, (x - hi.astype(F32)).astype(BF16)

def spline(s):
    a = jnp.abs(s)
    r = jnp.maximum(2.0 - a, 0.0)
    q = jnp.maximum(1.0 - a, 0.0)
    return (r * r * r - 4.0 * (q * q * q)) * (1.0 / 6.0)

def date_of(r):
    rr = jnp.where(r < EVEN, r, r - EVEN)
    base = ((rr >> 4) << 5) + (rr & 15)
    return jnp.where(r < EVEN, base, base + 16)

def iota(shape, dim):
    return lax.broadcasted_iota(jnp.int32, shape, dim)

def block_inverse(c):
    n = c.shape[1]
    row = iota((1, n, n), 1)
    col = iota((1, n, n), 2)
    for j in range(n):
        prow = c[:, j:j + 1, :]
        pcol = c[:, :, j:j + 1]
        d = 1.0 / c[:, j:j + 1, j:j + 1]
        newrow = jnp.where(col[:, :1, :] == j, 1.0, prow) * d
        base = jnp.where(col == j, 0.0, c)
        c = jnp.where(row == j, newrow, base - pcol * newrow)
    return c

def newton(mats, floors, steps):
    xs, lows = [], []
    for m, floor in zip(mats, floors):
        n = m.shape[0]
        top = jnp.max(jnp.sum(jnp.abs(m), axis=1, keepdims=True), axis=0, keepdims=True)
        eye = (iota((n, n), 0) == iota((n, n), 1)).astype(F32)
        xs.append(eye * (2.0 / (top + floor)))
        lows.append(2.0 * floor / (top + floor))
    def body(_, carry):
        xs, lows = carry
        nx, nl = [], []
        ys = [nn(m, x, HI) for m, x in zip(mats, xs)]
        for x, y, low in zip(xs, ys, lows):
            n = x.shape[0]
            ab = low * (2.0 - low)
            k = 2.0 / (1.0 + ab)
            eye2 = jnp.where(iota((n, n), 0) == iota((n, n), 1), 2.0, 0.0)
            nx.append(nn(x, eye2 - y, HI) * k)
            nl.append(ab * k)
        return nx, nl
    xs, lows = lax.fori_loop(0, steps, body, (xs, lows))
    return xs

def own_dates(pair):
    row, col = iota((OWN, DATES), 0), iota((OWN, DATES), 1)
    return jnp.where((pair * 38 + row == date_of(col)) & (row < 38), 1.0, 0.0)

def setup_math(pd, w, pair):
    t = date_of(iota((DATES, KP), 0))
    at = (jnp.where(t == pd[1:2, :], 1.0, 0.0) - jnp.where(t == pd[0:1, :], 1.0, 0.0))
    at16 = at.astype(BF16)
    tt = date_of(iota((DATES, NB), 0)).astype(F32) * ((NB - 3.0) / (DATES - 1.0))
    temporal = spline(tt - (iota((DATES, NB), 1).astype(F32) - 1.0))
    t1 = temporal.T
    a = t1.astype(BF16); r = t1 - a.astype(F32)
    b = r.astype(BF16); c = (r - b.astype(F32)).astype(BF16)
    xt = nn(a, at16) + nn(b, at16) + nn(c, at16)
    xs, ys, es, ns = [], [], [], []
    pis = []
    eyeN = jnp.where(iota((DATES, DATES), 0) == iota((DATES, DATES), 1), 1.0, 0.0)
    fold = jnp.where((iota((EVEN, 16), 0) & 15) == iota((EVEN, 16), 1), 1.0, 0.0)
    blockmask = (iota((EVEN, EVEN), 0) >> 4) == (iota((EVEN, EVEN), 1) >> 4)
    comps = []
    fn = []
    for i in range(2):
        wi = w[i:i + 1, :]
        whi, wlo = split2(wi)
        n = nt((at * whi.astype(F32)).astype(BF16), at16) + nt((at * wlo.astype(F32)).astype(BF16), at16) + eyeN
        ns.append(n)
        p = n[:EVEN, :EVEN]
        comps.append(nn(jnp.where(blockmask, p, 0.0), fold, HI).reshape(10, 16, 16))
        fn.append(nt(xt * wi, xt, HI) + 0.5 * jnp.where(iota((NB, NB), 0) == iota((NB, NB), 1), 1.0, 0.0))
    inv = block_inverse(jnp.concatenate(comps, axis=0))
    schurs, yy = [], []
    for i in range(2):
        ci = inv[10 * i:10 * i + 10].reshape(EVEN, 16)
        pi = jnp.where(blockmask, nt(ci, fold, HI), 0.0)
        e = ns[i][:EVEN, EVEN:]
        y = nn(pi, e, HI)
        s = ns[i][EVEN:, EVEN:] - lax.dot_general(e, y, (((0,), (0,)), ((), ())), precision=HI, preferred_element_type=F32)
        pis.append(pi); yy.append(y); schurs.append(s)
    s0, s1, f0, f1 = newton([schurs[0], schurs[1], fn[0], fn[1]], [1.0, 1.0, 0.5, 0.5], 11)
    fs = [nn(f0, xt * w[0:1, :], HI).astype(BF16), nn(f1, xt * w[1:2, :], HI).astype(BF16)]
    out = []
    sel = own_dates(pair)
    ninv = []
    for i, si in enumerate((s0, s1)):
        ysi = nn(yy[i], si, HI)
        tl = pis[i] + nt(ysi, yy[i], HI)
        top = jnp.concatenate([tl, -ysi], axis=1)
        bot = jnp.concatenate([-ysi.T, si], axis=1)
        ninv.append(jnp.concatenate([top, bot], axis=0))
    def dsolve(m, wi):
        hi, lo = split2(m)
        return ((nn(hi, at16) + nn(lo, at16)) * wi).astype(BF16)
    d0 = dsolve(ninv[0], w[0:1, :])
    d1 = dsolve(nn(sel, ninv[1], HI), w[1:2, :])
    xhi, xlo = split2(xt)
    c0 = nt(d0, xhi) + nt(d0, xlo)
    c1 = nt(d1, xhi) + nt(d1, xlo)
    fa1 = nt(fs[1], at16)
    da1 = nt(d1, at16)
    lhs = jnp.concatenate([fs[0], fs[1], d0, d1], axis=0)
    return lhs, c0, c1, fa1, da1, sel

def tail_math(lhs, c0, c1, fa1, da1, sel, zall, g):
    (h,) = newton([g], [1.0], 12)
    zhi, zlo = split2(zall)
    lz = nn(lhs, zhi) + nn(lhs, zlo)
    f0z, f1z, d0z, d1z = lz[0:32], lz[32:64], lz[64:64 + DATES], lz[64 + DATES:]
    w0 = d0z - nn(c0, f0z, HI)
    s1 = nn(w0, h, HI)
    v = w0 - s1
    fz1 = f1z - nn(fa1, v, HI)
    dz1 = d1z - nn(da1, v, HI)
    w1 = dz1 - nn(c1, fz1, HI)
    s2 = nn(sel, s1, HI) + nn(w1, h, HI)
    e = nn(fa1, s1, HI)
    return e, s2


def setup_kernel(pd_ref, w_ref, lhs_ref, c0_ref, c1_ref, fa1_ref, da1_ref):
    lhs, c0, c1, fa1, da1, _ = setup_math(pd_ref[...], w_ref[...], lax.axis_index("pair"))
    lhs_ref[...] = lhs
    c0_ref[...] = c0
    c1_ref[...] = c1
    fa1_ref[...] = fa1
    da1_ref[...] = da1


def device_of(index):
    return (index // N_TILE, index % N_TILE)


def exchange_kernel(
    ph_ref, ck_ref, y_ref, z_ref, g_ref,
    ypad, cscr, bscr, lscr, zown, gown,
    c_send, c_recv, y_send, y_recv, z_send, z_recv, g_send, g_recv, own_sem,
):
    pair, tile = lax.axis_index("pair"), lax.axis_index("tile")
    me = pair * N_TILE + tile

    def peer(i):
        return lax.rem(me + i, DEVICES)

    barrier = pltpu.get_barrier_semaphore()

    def greet(i, _):
        pl.semaphore_signal(barrier, inc=1, device_id=device_of(peer(i)), device_id_type=MESH)
        return 0

    lax.fori_loop(1, DEVICES, greet, 0)
    pl.semaphore_wait(barrier, DEVICES - 1)

    def c_copy(other, slot):
        return pltpu.make_async_remote_copy(
            src_ref=cscr.at[slot], dst_ref=cscr.at[slot],
            send_sem=c_send.at[other], recv_sem=c_recv.at[slot],
            device_id=device_of(other), device_id_type=MESH,
        )

    def y_copy(other, slot):
        return pltpu.make_async_remote_copy(
            src_ref=ypad.at[other], dst_ref=y_ref.at[slot],
            send_sem=y_send.at[other], recv_sem=y_recv.at[slot],
            device_id=device_of(other), device_id_type=MESH,
        )

    def z_copy(other, slot):
        return pltpu.make_async_remote_copy(
            src_ref=zown, dst_ref=z_ref.at[slot],
            send_sem=z_send.at[other], recv_sem=z_recv.at[slot],
            device_id=device_of(other), device_id_type=MESH,
        )

    def g_copy(other, slot):
        return pltpu.make_async_remote_copy(
            src_ref=gown, dst_ref=g_ref.at[slot],
            send_sem=g_send.at[other], recv_sem=g_recv.at[slot],
            device_id=(pair, other), device_id_type=MESH,
        )

    cscr[me] = ck_ref[...]

    def c_start(i, _):
        c_copy(peer(i), me).start()
        return 0

    lax.fori_loop(1, DEVICES, c_start, 0)

    def y_pack(other):
        block = ph_ref[:, pl.ds(pl.multiple_of(other * PIX, PIX), PIX)]
        ypad[other] = jnp.concatenate([block, jnp.zeros((SLOTS - PAIRS, PIX), BF16)], axis=0)

    def y_start(i, _):
        other = peer(i)
        y_pack(other)
        y_copy(other, me).start()
        return 0

    lax.fori_loop(1, DEVICES, y_start, 0)
    y_pack(me)
    own = pltpu.make_async_copy(ypad.at[me], y_ref.at[me], own_sem)
    own.start()

    shift = tile.astype(F32) - 1.0
    centers = iota((KNOTS, 1), 0).astype(F32) - 1.0

    def build(slot_of, buf):
        lscr[buf, 0:16] = ypad[slot_of]
        for i in range(PIX // 128):
            lanes = pl.ds(i * 128, 128)
            code = cscr[slot_of, i:i + 1, :]
            row = (code >> 16).astype(F32) * ((KNOTS - 3.0) / FRAME)
            col = (code & 65535).astype(F32) * ((KNOTS - 3.0) / FRAME)
            rows = spline(row - centers)
            cols = spline(col - centers)
            for m in range(KNOTS):
                bscr[buf, m * KNOTS:(m + 1) * KNOTS, lanes] = (rows[m:m + 1, :] * cols).astype(BF16)
            mine = spline(row - shift) * cols
            hi, lo = split2(mine)
            lscr[buf, 16:32, lanes] = hi
            lscr[buf, 32:48, lanes] = lo

    def c_wait(i):
        other = peer(i)
        c_copy(other, other).wait_recv()

    def product(buf):
        return nt(lscr[buf], bscr[buf])

    build(me, 0)

    def pass_body(k, acc):
        c_wait(2 * k + 1)
        c_wait(2 * k + 2)
        build(peer(2 * k + 1), 1)
        acc = acc + product(0)
        build(peer(2 * k + 2), 0)
        return acc + product(1)

    acc = lax.fori_loop(0, DEVICES // 2 - 1, pass_body, jnp.zeros((48, SCREEN), F32))
    c_wait(DEVICES - 1)
    build(peer(DEVICES - 1), 1)
    acc = acc + product(0)
    acc = acc + product(1)

    zown[...] = acc[0:16]
    gown[...] = acc[16:48]

    def z_start(i, _):
        z_copy(peer(i), me).start()
        return 0

    lax.fori_loop(1, DEVICES, z_start, 0)

    def g_start(i, _):
        g_copy(lax.rem(tile + i, N_TILE), tile).start()
        return 0

    lax.fori_loop(1, N_TILE, g_start, 0)
    z_ref[me] = acc[0:16]
    g_ref[tile] = acc[16:48]

    def g_wait(i, _):
        other = lax.rem(tile + i, N_TILE)
        g_copy(other, other).wait_recv()
        g_copy(other, tile).wait_send()
        return 0

    lax.fori_loop(1, N_TILE, g_wait, 0)

    def z_wait(i, _):
        other = peer(i)
        z_copy(other, other).wait_recv()
        z_copy(other, me).wait_send()
        c_copy(other, me).wait_send()
        return 0

    lax.fori_loop(1, DEVICES, z_wait, 0)

    def y_wait(i, _):
        other = peer(i)
        y_copy(other, other).wait_recv()
        y_copy(other, me).wait_send()
        return 0

    lax.fori_loop(1, DEVICES, y_wait, 0)
    own.wait()


def final_kernel(lhs_ref, c0_ref, c1_ref, fa1_ref, da1_ref, z_ref, g_ref, y_ref, ck_ref, co_ref, sc_ref, bscr):
    pair = lax.axis_index("pair")
    first = jnp.concatenate([g_ref[j, 0:16] for j in range(KNOTS)], axis=0)
    second = jnp.concatenate([g_ref[j, 16:32] for j in range(KNOTS)], axis=0)
    eye = jnp.where(iota((SCREEN, SCREEN), 0) == iota((SCREEN, SCREEN), 1), 1.0, 0.0)
    gram = first + second + second.T + eye
    sel = own_dates(pair)
    e, s2 = tail_math(
        lhs_ref[...], c0_ref[...], c1_ref[...], fa1_ref[...], da1_ref[...], sel,
        z_ref[...].reshape(KP, SCREEN), gram,
    )
    sc_ref[...] = s2[0:38]
    centers = iota((KNOTS, 1), 0).astype(F32) - 1.0
    for i in range(PIX // 128):
        lanes = pl.ds(i * 128, 128)
        code = ck_ref[i:i + 1, :]
        row = (code >> 16).astype(F32) * ((KNOTS - 3.0) / FRAME)
        col = (code & 65535).astype(F32) * ((KNOTS - 3.0) / FRAME)
        rows = spline(row - centers)
        cols = spline(col - centers)
        for m in range(KNOTS):
            bscr[m * KNOTS:(m + 1) * KNOTS, lanes] = (rows[m:m + 1, :] * cols).astype(BF16)
    ehi, elo = split2(e)
    screen_part = nn(ehi, bscr[...]) + nn(elo, bscr[...])
    fit = nn(lhs_ref[32:64, :], y_ref[...].reshape(KP, PIX))
    co_ref[...] = fit - screen_part


def local(phases, pair_dates, weights, coords):
    pd = jnp.pad(pair_dates.reshape(DEVICES, PAIRS, 2), ((0, 0), (0, SLOTS - PAIRS), (0, 0)), constant_values=-1)
    pd = pd.reshape(KP, 2).T
    w = jnp.pad(weights.reshape(2, DEVICES, PAIRS), ((0, 0), (0, 0), (0, SLOTS - PAIRS))).reshape(2, KP)
    codes = (coords[0] * 65536 + coords[1]).reshape(PIX // 128, 128)
    vmem = pl.BlockSpec(memory_space=pltpu.VMEM)
    anyspace = pl.BlockSpec(memory_space=pl.ANY)
    shape = jax.ShapeDtypeStruct
    lhs, c0, c1, fa1, da1 = pl.pallas_call(
        setup_kernel,
        out_shape=[
            shape((2 * NB + DATES + OWN, KP), BF16), shape((DATES, NB), F32), shape((OWN, NB), F32),
            shape((NB, DATES), F32), shape((OWN, DATES), F32),
        ],
        in_specs=[vmem] * 2,
        out_specs=[vmem] * 5,
        compiler_params=pltpu.CompilerParams(vmem_limit_bytes=VMEM_LIMIT),
        name="setup",
    )(pd, w)
    dma = pltpu.SemaphoreType.DMA
    y, z, g = pl.pallas_call(
        exchange_kernel,
        out_shape=[
            shape((DEVICES, SLOTS, PIX), BF16), shape((DEVICES, SLOTS, SCREEN), F32),
            shape((N_TILE, 32, SCREEN), F32),
        ],
        in_specs=[vmem] * 2,
        out_specs=[anyspace, vmem, vmem],
        scratch_shapes=[
            pltpu.VMEM((DEVICES, SLOTS, PIX), BF16),
            pltpu.VMEM((DEVICES, PIX // 128, 128), jnp.int32),
            pltpu.VMEM((2, SCREEN, PIX), BF16),
            pltpu.VMEM((2, 48, PIX), BF16),
            pltpu.VMEM((SLOTS, SCREEN), F32),
            pltpu.VMEM((32, SCREEN), F32),
            dma((DEVICES,)), dma((DEVICES,)), dma((DEVICES,)), dma((DEVICES,)),
            dma((DEVICES,)), dma((DEVICES,)), dma((N_TILE,)), dma((N_TILE,)), dma,
        ],
        compiler_params=pltpu.CompilerParams(
            collective_id=0, has_side_effects=True, vmem_limit_bytes=VMEM_LIMIT
        ),
        name="exchange",
    )(phases, codes)
    co, sc = pl.pallas_call(
        final_kernel,
        out_shape=[shape((NB, PIX), F32), shape((38, SCREEN), F32)],
        in_specs=[vmem] * 9,
        out_specs=[vmem] * 2,
        scratch_shapes=[pltpu.VMEM((SCREEN, PIX), BF16)],
        compiler_params=pltpu.CompilerParams(vmem_limit_bytes=VMEM_LIMIT),
        name="final",
    )(lhs, c0, c1, fa1, da1, z, g, y, codes)
    return co, sc


def solution(mesh):
    return jax.shard_map(
        local,
        mesh=mesh,
        in_specs=(P(("pair", "tile"), None), P(), P(), P(None, ("pair", "tile"))),
        out_specs=(P(None, ("pair", "tile")), P("pair", None)),
        check_vma=False,
    )
```

time: 704 us -> 185 us (0.26)
  waiting for transfers between devices: 287 us -> 0 us
  other arithmetic: 252 us -> 1.38 us
  Pallas kernels: 0 us -> 179 us
  matrix products: 83.5 us -> 0 us
  local copies, waits for them, and re-layouts: 42.3 us -> 3.17 us
  between operations: 20.2 us -> 0.67 us
  starting transfers between devices: 12.4 us -> 0 us
    psum x2 -> x0, waiting for transfers between devices: 287 us -> none  [local(): totals = lax.psum(partial_value, ('pair', 'tile'))]
    another operation x49 -> x0, other arithmetic: 233 us -> none  [the longest x20 98.1 us: pair_setup(): date_factor = jnp.linalg.cholesky(date_normal)]
    pallas_call x0 -> x3, Pallas kernels: none -> 179 us  [the longest x1 132 us: local(): pl.pallas_call(exchange_kernel, out_shape=[shape((DEVICES, SLOTS, PIX), B...]
    another operation x46 -> x0, matrix products: 46 us -> none  [the longest x20 28.7 us: pair_setup(): jax.scipy.linalg.cho_solve((date_factor, True), weighted.T)]
    dot_general x13 -> x0, matrix products: 37.5 us -> none  [the longest x2 12 us: pair_setup(): jnp.dot(incidence.T, weighted, precision=lax.Precision.HIGHEST)]
    another operation x32 -> x0, local copies, waits for them, and re-layouts: 13.3 us -> none  [the longest x14 9.15 us: pair_setup(): jax.scipy.linalg.cho_solve((date_factor, True), weighted.T)]
    all_to_all x1 -> x0, starting transfers between devices: 11.9 us -> none  [local(): lax.all_to_all(shaped, ('pair', 'tile'), split_axis=1, concat_axis=0, til...]
    gather x2 -> x0, local copies, waits for them, and re-layouts: 11.7 us -> none  [the longest x1 5.84 us: local(): jnp.take(screen_field, pair_dates[:, 1], axis=0)]
  transfers between devices with their start and end apart: 3 -> 0, of which waited for: 2 -> 0; matrix products, arithmetic and copies ran while one was open for 37% -> 0% of each run, Pallas kernels for 0% -> 0%
where the time goes in v1:
time: 185 us
  Pallas kernels  179 us (97%)
  local copies, waits for them, and re-layouts  3.17 us (2%)
    pallas_call x1, Pallas kernels, local(): pl.pallas_call(exchange_kernel, out_shape=[shape((DEVICES, SLOTS, PIX), B...  132 us
    pallas_call x1, Pallas kernels, local(): pl.pallas_call(final_kernel, out_shape=[shape((NB, PIX), F32), shape((38,...  23.6 us
    pallas_call x1, Pallas kernels, local(): pl.pallas_call(setup_kernel, out_shape=[shape((2 * NB + DATES + OWN, KP),...  23.6 us

profile of v1, /device:TPU:1, one launch (start us, length us, event | category | flops | bytes accessed | tf_op | source)
XLA Modules:
  0.0 184.5 jit_solution(5520411192181759676)
XLA Ops:
  0.6 1.4 slice_add_fusion
  2.0 0.9 reshape.22
  2.9 0.7 reshape.23
  3.6 0.9 reshape.24
  4.5 0.7 reshape.25.w_ref
  5.2 23.6 %setup.1 = (bf16[408,2048]{1,0:T(8,128)(2,1)}, f32[304,32]{1,0:T(8,128)}, f32[40,32]{1,0:T(8,128)}, f32[32,304]{1,0:T(8,128)}, f32[40,304]{1,0:T(8,128)}) custom-call(s32[2,2048]{1,0:T(2,128)} %bitcast.6, f32[2,2048]{1,0:T(2,128)} %reshape.25.w_ref), custom_call_target="tpu_custom_call" | custom-call | tf_op jit(solution)/shard_map/setup/pallas_call | solution.py:365
  28.9 132.0 %exchange.1 = (bf16[128,16,1024]{2,1,0:T(8,128)(2,1)}, f32[128,16,256]{2,1,0:T(8,128)}, f32[16,32,256]{2,1,0:T(8,128)}) custom-call(bf16[12,131072]{1,0:T(8,128)(2,1)} %ph_ref.1, s32[8,128]{1,0:T(8,128)} %bitcast.7), custom_call_target="tpu_custom_call" | custom-call | tf_op jit(solution)/shard_map/exchange/pallas_call | solution.py:377
  160.9 23.6 %final.1 = (f32[32,1024]{1,0:T(8,128)}, f32[38,256]{1,0:T(8,128)}) custom-call(bf16[408,2048]{1,0:T(8,128)(2,1)} %get-tuple-element.10.lhs_ref, f32[304,32]{1,0:T(8,128)} %get-tuple-element.11.c0_ref, f32[40,32]{1,0:T(8,128)} %get-tuple-element.12.c1_ref, f32[32,304]{1,0:T(8,128)} %get-tuple-element.13.fa1_ref, f32[40,304]{1,0:T(8,128)} %get-tuple-element.14.da1_ref, ...), custom_call_target="tpu_custom_call" | custom-call | tf_op jit(solution)/shard_map/final/pallas_call | solution.py:400
  (2 shorter events, 0.0 us)

commit v2 on v0

v2 whole, which is shorter than its diff:
```python
import functools

import jax
import jax.numpy as jnp
from jax import lax
from jax.experimental import pallas as pl
from jax.experimental.pallas import tpu as pltpu
from jax.sharding import PartitionSpec as P

MESH = pl.DeviceIdType.MESH
HI = lax.Precision.HIGHEST
F32, BF16 = jnp.float32, jnp.bfloat16
DATES, NB, KNOTS, FRAME, SCREEN = 304, 32, 16, 4096, 256
PAIRS, SLOTS, DEVICES, PIX = 12, 16, 128, 1024
N_TILE = 16
EVEN, ODD = 160, 144
KP = SLOTS * DEVICES
OWN = 40
N_PAIR = 8
F0_AT, F1_AT, D1_AT, ROWS = 384, 416, 448, 512
VMEM_LIMIT = 60 * 1024 * 1024

def nn(a, b, precision=None):
    return lax.dot_general(a, b, (((1,), (0,)), ((), ())), precision=precision, preferred_element_type=F32)

def nt(a, b, precision=None):
    return lax.dot_general(a, b, (((1,), (1,)), ((), ())), precision=precision, preferred_element_type=F32)

def tn(a, b, precision=None):
    return lax.dot_general(a, b, (((0,), (0,)), ((), ())), precision=precision, preferred_element_type=F32)

def split2(x):
    hi = x.astype(BF16)
    return hi, (x - hi.astype(F32)).astype(BF16)

def spline(s):
    a = jnp.abs(s)
    r = jnp.maximum(2.0 - a, 0.0)
    q = jnp.maximum(1.0 - a, 0.0)
    return (r * r * r - 4.0 * (q * q * q)) * (1.0 / 6.0)

def date_of(r):
    rr = jnp.where(r < EVEN, r, r - EVEN)
    base = ((rr >> 4) << 5) + (rr & 15)
    return jnp.where(r < EVEN, base, base + 16)

def iota(shape, dim):
    return lax.broadcasted_iota(jnp.int32, shape, dim)

def block_inverse(c):
    n = c.shape[1]
    row = iota((1, n, n), 1)
    col = iota((1, n, n), 2)
    for j in range(n):
        prow = c[:, j:j + 1, :]
        pcol = c[:, :, j:j + 1]
        d = 1.0 / c[:, j:j + 1, j:j + 1]
        newrow = jnp.where(col[:, :1, :] == j, 1.0, prow) * d
        base = jnp.where(col == j, 0.0, c)
        c = jnp.where(row == j, newrow, base - pcol * newrow)
    return c

def product3(a, b):
    (ah, al), (bh, bl) = a, b
    return nn(ah, bh) + (nn(ah, bl) + nn(al, bh))

def newton(mats, floors, steps):
    xs, lows, parts, eyes = [], [], [], []
    for m, floor in zip(mats, floors):
        n = m.shape[0]
        top = jnp.max(jnp.sum(jnp.abs(m), axis=1, keepdims=True), axis=0, keepdims=True)
        diagonal = iota((n, n), 0) == iota((n, n), 1)
        xs.append(jnp.where(diagonal, 2.0 / (top + floor), 0.0))
        lows.append(2.0 * floor / (top + floor))
        parts.append(split2(m))
        eyes.append(jnp.where(diagonal, 2.0, 0.0))
    def body(_, carry):
        xs, lows = carry
        nx, nl = [], []
        halves = [split2(x) for x in xs]
        ys = [product3(m, x) for m, x in zip(parts, halves)]
        for x, y, eye, low in zip(halves, ys, eyes, lows):
            ab = low * (2.0 - low)
            k = 2.0 / (1.0 + ab)
            nx.append(product3(x, split2(eye - y)) * k)
            nl.append(ab * k)
        return nx, nl
    xs, lows = lax.fori_loop(0, steps, body, (xs, lows))
    out = []
    for m, x, eye in zip(mats, xs, eyes):
        out.append(nn(x, eye - nn(m, x, HI), HI))
    return out

def own_dates(pair):
    row, col = iota((OWN, DATES), 0), iota((OWN, DATES), 1)
    return jnp.where((pair * 38 + row == date_of(col)) & (row < 38), 1.0, 0.0)

def incidence_rows(pd):
    t = date_of(iota((DATES, KP), 0))
    later = jnp.where(t == pd[1:2, :], 1.0, 0.0)
    return later - jnp.where(t == pd[0:1, :], 1.0, 0.0)

def design_rows(at16):
    tt = date_of(iota((DATES, NB), 0)).astype(F32) * ((NB - 3.0) / (DATES - 1.0))
    t1 = spline(tt - (iota((DATES, NB), 1).astype(F32) - 1.0)).T
    a = t1.astype(BF16)
    r = t1 - a.astype(F32)
    b, c = split2(r)
    return nn(a, at16) + nn(b, at16) + nn(c, at16)

def normal_parts(at, at16, xt, w):
    eye = jnp.where(iota((DATES, DATES), 0) == iota((DATES, DATES), 1), 1.0, 0.0)
    fold = jnp.where((iota((EVEN, 16), 0) & 15) == iota((EVEN, 16), 1), 1.0, 0.0)
    mask = (iota((EVEN, EVEN), 0) >> 4) == (iota((EVEN, EVEN), 1) >> 4)
    ns, comps, fits = [], [], []
    for i in range(2):
        wi = w[i:i + 1, :]
        hi, lo = split2(wi)
        n = nt((at * hi.astype(F32)).astype(BF16), at16) + nt((at * lo.astype(F32)).astype(BF16), at16) + eye
        ns.append(n)
        comps.append(nn(jnp.where(mask, n[:EVEN, :EVEN], 0.0), fold, HI).reshape(10, 16, 16))
        fits.append(nt(xt * wi, xt, HI) + jnp.where(iota((NB, NB), 0) == iota((NB, NB), 1), 0.5, 0.0))
    inv = block_inverse(jnp.concatenate(comps, axis=0))
    firsts, links, schurs = [], [], []
    for i in range(2):
        compact = inv[10 * i:10 * i + 10].reshape(EVEN, 16)
        first = jnp.where(mask, nt(compact, fold, HI), 0.0)
        e = ns[i][:EVEN, EVEN:]
        y = nn(first, e, HI)
        schurs.append(ns[i][EVEN:, EVEN:] - tn(e, y, HI))
        firsts.append(first)
        links.append(y)
    return firsts, links, schurs, fits

def full_inverse(first, link, last):
    right = nn(link, last, HI)
    top = jnp.concatenate([first + nt(right, link, HI), -right], axis=1)
    bottom = jnp.concatenate([-right.T, last], axis=1)
    return jnp.concatenate([top, bottom], axis=0)

def date_solve(inverse, at16, wi):
    hi, lo = split2(inverse)
    return ((nn(hi, at16) + nn(lo, at16)) * wi).astype(BF16)

def knot_rows(code, centers):
    scale = (KNOTS - 3.0) / FRAME
    rows = spline((code >> 16).astype(F32) * scale - centers)
    cols = spline((code & 65535).astype(F32) * scale - centers)
    return rows, cols


def mega_kernel(
    ph_ref, ck_ref, pd_ref, w_ref, co_ref, sc_ref,
    cg, sb, rb, bhi, blo_ref, ybuf, gs, gr, gg, zs, zr, zg, wg, cp, cr, lhs,
    c_send, c_recv, y_send, y_recv, gs_send, gs_recv, gg_send, gg_recv,
    zs_send, zs_recv, zg_send, zg_recv, w_send, w_recv, f_send, f_recv,
):
    pair, tile = lax.axis_index("pair"), lax.axis_index("tile")

    def tile_peer(i):
        return lax.rem(tile + i, N_TILE)

    def pair_peer(i):
        return lax.rem(pair + i, N_PAIR)

    def loop(lo, hi, f):
        def body(i, carry):
            f(i)
            return carry
        lax.fori_loop(lo, hi, body, 0)

    def to_tile(src, dst, send, recv, other, slot):
        return pltpu.make_async_remote_copy(
            src_ref=src, dst_ref=dst.at[slot], send_sem=send.at[other], recv_sem=recv.at[slot],
            device_id=(pair, other), device_id_type=MESH,
        )

    def to_pair(src, dst, send, recv, other, slot):
        return pltpu.make_async_remote_copy(
            src_ref=src, dst_ref=dst.at[slot], send_sem=send.at[other], recv_sem=recv.at[slot],
            device_id=(other, tile), device_id_type=MESH,
        )

    def c_copy(other, slot):
        return to_pair(cg.at[pair], cg, c_send, c_recv, other, slot)

    def y_copy(other, slot):
        return to_tile(sb.at[other], rb, y_send, y_recv, other, slot)

    def gs_copy(other, slot):
        return to_tile(gs.at[other], gr, gs_send, gs_recv, other, slot)

    def gg_copy(other, slot):
        return to_tile(gg.at[tile], gg, gg_send, gg_recv, other, slot)

    def zs_copy(other, slot):
        return to_tile(zs.at[other], zr, zs_send, zs_recv, other, slot)

    def zg_copy(other, slot):
        return to_pair(zg.at[pair], zg, zg_send, zg_recv, other, slot)

    def w_copy(other, slot):
        return to_tile(wg.at[tile], wg, w_send, w_recv, other, slot)

    def f_copy(other, slot):
        return to_pair(cp.at[other], cr, f_send, f_recv, other, slot)

    def start_tile(copy):
        loop(1, N_TILE, lambda i: copy(tile_peer(i), tile).start())

    def start_pair(copy):
        loop(1, N_PAIR, lambda i: copy(pair_peer(i), pair).start())

    def wait_tile(copy):
        loop(1, N_TILE, lambda i: copy(tile_peer(i), tile_peer(i)).wait_recv())

    def wait_pair(copy):
        loop(1, N_PAIR, lambda i: copy(pair_peer(i), pair_peer(i)).wait_recv())

    barrier = pltpu.get_barrier_semaphore()
    loop(1, N_TILE, lambda i: pl.semaphore_signal(
        barrier, inc=1, device_id=(pair, tile_peer(i)), device_id_type=MESH))
    loop(1, N_PAIR, lambda i: pl.semaphore_signal(
        barrier, inc=1, device_id=(pair_peer(i), tile), device_id_type=MESH))
    pl.semaphore_wait(barrier, N_TILE + N_PAIR - 2)

    cg[pair] = ck_ref[...]
    start_pair(c_copy)

    def pack(other, dst):
        blocks = []
        for p in range(N_PAIR):
            first = pl.multiple_of((p * N_TILE + other) * PIX, PIX)
            blocks.append(ph_ref[:, pl.ds(first, PIX)].astype(F32))
        for a in range(4):
            two = jnp.concatenate([blocks[2 * a][0:8], blocks[2 * a + 1][0:8]], axis=0)
            dst[a] = two.astype(BF16)
        for a in range(2):
            four = jnp.concatenate([blocks[4 * a + q][8:12] for q in range(4)], axis=0)
            dst[4 + a] = four.astype(BF16)

    def y_start(i):
        other = tile_peer(i)
        pack(other, sb.at[other])
        y_copy(other, tile).start()

    loop(1, N_TILE, y_start)
    pack(tile, rb.at[tile])

    wait_pair(c_copy)
    centers = iota((KNOTS, 1), 0).astype(F32) - 1.0

    def knots(p, carry):
        g1, g2 = carry
        for i in range(PIX // 128):
            rows, cols = knot_rows(cg[p, i:i + 1, :], centers)
            lanes = pl.ds(i * 128, 128)
            for m in range(KNOTS):
                hi, lo = split2(rows[m:m + 1, :] * cols)
                bhi[p, m * KNOTS:(m + 1) * KNOTS, lanes] = hi
                blo_ref[m * KNOTS:(m + 1) * KNOTS, lanes] = lo
        hi = bhi[p]
        return g1 + nt(hi, hi), g2 + nt(hi, blo_ref[...])

    zero = jnp.zeros((SCREEN, SCREEN), F32)
    g1, g2 = lax.fori_loop(0, N_PAIR, knots, (zero, zero))
    gpart = (g1 + g2 + g2.T).reshape(N_TILE, KNOTS, SCREEN)
    gs[...] = gpart
    start_tile(gs_copy)
    gr[tile] = gs[tile]

    w = w_ref[...]
    at = incidence_rows(pd_ref[...])
    at16 = at.astype(BF16)
    xt = design_rows(at16)
    firsts, links, schurs, fits = normal_parts(at, at16, xt, w)

    wait_tile(gs_copy)
    gsum = gr[0]
    for t in range(1, N_TILE):
        gsum = gsum + gr[t]
    gg[tile] = gsum
    start_tile(gg_copy)
    wait_tile(gg_copy)
    gram = gg[...].reshape(SCREEN, SCREEN)
    gram = gram + jnp.where(iota((SCREEN, SCREEN), 0) == iota((SCREEN, SCREEN), 1), 1.0, 0.0)
    h, last0, last1, f0, f1 = newton([gram] + schurs + fits, [1.0, 1.0, 1.0, 0.5, 0.5], 11)
    sel = own_dates(pair)
    fit0 = nn(f0, xt * w[0:1, :], HI).astype(BF16)
    fit1 = nn(f1, xt * w[1:2, :], HI).astype(BF16)
    d0 = date_solve(full_inverse(firsts[0], links[0], last0), at16, w[0:1, :])
    d1 = date_solve(nn(sel, full_inverse(firsts[1], links[1], last1), HI), at16, w[1:2, :])
    lhs[0:DATES] = d0
    lhs[DATES:F0_AT] = jnp.zeros((F0_AT - DATES, KP), BF16)
    lhs[F0_AT:D1_AT] = jnp.concatenate([fit0, fit1], axis=0)
    lhs[D1_AT:ROWS] = jnp.concatenate([d1, jnp.zeros((ROWS - D1_AT - OWN, KP), BF16)], axis=0)
    xhi, xlo = split2(xt)
    c0 = nt(d0, xhi) + nt(d0, xlo)
    c1 = nt(d1, xhi) + nt(d1, xlo)
    fa1 = nt(fit1, at16)
    da1 = nt(d1, at16)

    def unpack(t):
        rest = [rb[t, 4 + a].astype(F32) for a in range(2)]
        for a in range(4):
            two = rb[t, a].astype(F32)
            for b in range(2):
                p = 2 * a + b
                low = rest[p // 4][4 * (p % 4):4 * (p % 4) + 4]
                block = jnp.concatenate([two[8 * b:8 * b + 8], low, jnp.zeros((4, PIX), F32)], axis=0)
                rows = pl.ds(pl.multiple_of(t * SLOTS, SLOTS), SLOTS)
                ybuf[p, rows, :] = block.astype(BF16)

    unpack(tile)

    def y_arrive(i):
        other = tile_peer(i)
        y_copy(other, other).wait_recv()
        unpack(other)

    loop(1, N_TILE, y_arrive)
    fit_own = lhs[F1_AT:D1_AT, pl.ds(pl.multiple_of(pair * SCREEN, SCREEN), SCREEN)]

    def z_body(p, acc):
        y = ybuf[p]
        cp[p] = nn(fit_own, y)
        return acc + nt(bhi[p], y)

    zt = lax.fori_loop(0, N_PAIR, z_body, zero)
    zs[...] = zt.reshape(N_TILE, KNOTS, SCREEN)
    start_tile(zs_copy)
    start_pair(f_copy)
    zr[tile] = zs[tile]
    cr[pair] = cp[pair]
    wait_tile(zs_copy)
    zsum = zr[0]
    for t in range(1, N_TILE):
        zsum = zsum + zr[t]
    zg[pair] = zsum
    start_pair(zg_copy)
    wait_pair(zg_copy)
    zrow = jnp.concatenate([zg[p] for p in range(N_PAIR)], axis=1)
    zhi, zlo = split2(zrow)
    both = nt(jnp.concatenate([zhi, zlo], axis=0), lhs[...])
    wg[tile] = both[0:KNOTS] + both[KNOTS:2 * KNOTS]
    start_tile(w_copy)
    wait_tile(w_copy)

    wt = wg[...].reshape(SCREEN, ROWS)
    w0 = wt[:, 0:DATES] - nt(wt[:, F0_AT:F1_AT], c0, HI)
    s1 = nn(h, w0, HI)
    e = nt(s1, fa1, HI).T
    v = w0 - s1
    fz1 = wt[:, F1_AT:D1_AT] - nt(v, fa1, HI)
    dz1 = wt[:, D1_AT:D1_AT + OWN] - nt(v, da1, HI)
    s2 = nt(s1, sel, HI) + nn(h, dz1 - nt(fz1, c1, HI), HI)
    sc_ref[...] = s2.T[0:38]
    wait_pair(f_copy)
    ehi, elo = split2(e)
    own_knots = bhi[pair]
    total = cr[0]
    for p in range(1, N_PAIR):
        total = total + cr[p]
    co_ref[...] = total - (nn(ehi, own_knots) + nn(elo, own_knots))

    def drain_tile(i):
        other = tile_peer(i)
        for copy in (y_copy, gs_copy, gg_copy, zs_copy, w_copy):
            copy(other, tile).wait_send()

    loop(1, N_TILE, drain_tile)

    def drain_pair(i):
        other = pair_peer(i)
        for copy in (c_copy, zg_copy, f_copy):
            copy(other, pair).wait_send()

    loop(1, N_PAIR, drain_pair)


def local(phases, pair_dates, weights, coords):
    pd = jnp.pad(pair_dates.reshape(DEVICES, PAIRS, 2), ((0, 0), (0, SLOTS - PAIRS), (0, 0)), constant_values=-1)
    pd = pd.reshape(KP, 2).T
    w = jnp.pad(weights.reshape(2, DEVICES, PAIRS), ((0, 0), (0, 0), (0, SLOTS - PAIRS))).reshape(2, KP)
    codes = (coords[0] * 65536 + coords[1]).reshape(PIX // 128, 128)
    vmem = pl.BlockSpec(memory_space=pltpu.VMEM)
    shape = jax.ShapeDtypeStruct
    dma = pltpu.SemaphoreType.DMA
    tiles, pairs = dma((N_TILE,)), dma((N_PAIR,))
    return pl.pallas_call(
        mega_kernel,
        out_shape=[shape((NB, PIX), F32), shape((38, SCREEN), F32)],
        in_specs=[vmem] * 4,
        out_specs=[vmem] * 2,
        scratch_shapes=[
            pltpu.VMEM((N_PAIR, PIX // 128, 128), jnp.int32),
            pltpu.VMEM((N_TILE, 6, SLOTS, PIX), BF16),
            pltpu.VMEM((N_TILE, 6, SLOTS, PIX), BF16),
            pltpu.VMEM((N_PAIR, SCREEN, PIX), BF16),
            pltpu.VMEM((SCREEN, PIX), BF16),
            pltpu.VMEM((N_PAIR, SCREEN, PIX), BF16),
            pltpu.VMEM((N_TILE, KNOTS, SCREEN), F32),
            pltpu.VMEM((N_TILE, KNOTS, SCREEN), F32),
            pltpu.VMEM((N_TILE, KNOTS, SCREEN), F32),
            pltpu.VMEM((N_TILE, KNOTS, SCREEN), F32),
            pltpu.VMEM((N_TILE, KNOTS, SCREEN), F32),
            pltpu.VMEM((N_PAIR, KNOTS, SCREEN), F32),
            pltpu.VMEM((N_TILE, KNOTS, ROWS), F32),
            pltpu.VMEM((N_PAIR, NB, PIX), F32),
            pltpu.VMEM((N_PAIR, NB, PIX), F32),
            pltpu.VMEM((ROWS, KP), BF16),
            pairs, pairs, tiles, tiles, tiles, tiles, tiles, tiles,
            tiles, tiles, pairs, pairs, tiles, tiles, pairs, pairs,
        ],
        compiler_params=pltpu.CompilerParams(
            collective_id=0, has_side_effects=True, vmem_limit_bytes=VMEM_LIMIT
        ),
        name="mega",
    )(phases, codes, pd, w)


def solution(mesh):
    return jax.shard_map(
        local,
        mesh=mesh,
        in_specs=(P(("pair", "tile"), None), P(), P(), P(None, ("pair", "tile"))),
        out_specs=(P(None, ("pair", "tile")), P("pair", None)),
        check_vma=False,
    )
```

time: 704 us -> 134 us (0.19)
  waiting for transfers between devices: 287 us -> 0 us
  other arithmetic: 252 us -> 1.36 us
  Pallas kernels: 0 us -> 125 us
  matrix products: 83.5 us -> 0 us
  local copies, waits for them, and re-layouts: 42.3 us -> 6.14 us
  between operations: 20.2 us -> 0.67 us
  starting transfers between devices: 12.4 us -> 0 us
    psum x2 -> x0, waiting for transfers between devices: 287 us -> none  [local(): totals = lax.psum(partial_value, ('pair', 'tile'))]
    another operation x49 -> x0, other arithmetic: 233 us -> none  [the longest x20 98.1 us: pair_setup(): date_factor = jnp.linalg.cholesky(date_normal)]
    pallas_call x0 -> x1, Pallas kernels: none -> 125 us  [local(): pl.pallas_call(mega_kernel, out_shape=[shape((NB, PIX), F32), shape((38,...]
    another operation x46 -> x0, matrix products: 46 us -> none  [the longest x20 28.7 us: pair_setup(): jax.scipy.linalg.cho_solve((date_factor, True), weighted.T)]
    dot_general x13 -> x0, matrix products: 37.5 us -> none  [the longest x2 12 us: pair_setup(): jnp.dot(incidence.T, weighted, precision=lax.Precision.HIGHEST)]
    another operation x32 -> x0, local copies, waits for them, and re-layouts: 13.3 us -> none  [the longest x14 9.15 us: pair_setup(): jax.scipy.linalg.cho_solve((date_factor, True), weighted.T)]
    all_to_all x1 -> x0, starting transfers between devices: 11.9 us -> none  [local(): lax.all_to_all(shaped, ('pair', 'tile'), split_axis=1, concat_axis=0, til...]
    gather x2 -> x0, local copies, waits for them, and re-layouts: 11.7 us -> none  [the longest x1 5.84 us: local(): jnp.take(screen_field, pair_dates[:, 1], axis=0)]
  transfers between devices with their start and end apart: 3 -> 0, of which waited for: 2 -> 0; matrix products, arithmetic and copies ran while one was open for 37% -> 0% of each run, Pallas kernels for 0% -> 0%
where the time goes in v2:
time: 134 us; the launch traced here: 133 us
  Pallas kernels  125 us (93%)
  local copies, waits for them, and re-layouts  6.14 us (5%)
  other arithmetic  1.36 us (1%)
    pallas_call x1, Pallas kernels, local(): pl.pallas_call(mega_kernel, out_shape=[shape((NB, PIX), F32), shape((38,...  125 us
    unnamed x2, local copies, waits for them, and re-layouts  2.97 us

profile of v2, /device:TPU:1, one launch (start us, length us, event | category | flops | bytes accessed | tf_op | source)
XLA Modules:
  0.0 133.5 jit_solution(1719273296419111278)
XLA Ops:
  0.6 1.4 %slice_add_fusion = s32[1,1024]{1,0:T(1,128)} fusion(s32[2,1024]{1,0:T(2,128)} %param.7), kind=kLoop, calls=%fused_computation | loop fusion | flops 2048 | bytes 12288 | tf_op jit(solution)/shard_map/add | solution.py:385
  2.0 0.9 reshape.22
  2.9 0.7 reshape.23
  3.6 0.9 reshape.24
  4.5 0.7 reshape.25.w_ref
  5.2 125.3 %mega.1 = (f32[32,1024]{1,0:T(8,128)}, f32[38,256]{1,0:T(8,128)}) custom-call(bf16[12,131072]{1,0:T(8,128)(2,1)} %ph_ref.1, s32[8,128]{1,0:T(8,128)} %bitcast.7, s32[2,2048]{1,0:T(2,128)} %bitcast.6, f32[2,2048]{1,0:T(2,128)} %reshape.25.w_ref), custom_call_target="tpu_custom_call" | custom-call | tf_op jit(solution)/shard_map/mega/pallas_call | solution.py:390
  130.5 1.6 %copy.8 = f32[32,1024]{1,0:T(8,128)} copy(f32[32,1024]{1,0:T(8,128)} %get-tuple-element.4) | data formatting | bytes 262144
  132.1 1.4 %copy.9 = f32[38,256]{1,0:T(8,128)} copy(f32[38,256]{1,0:T(8,128)} %get-tuple-element.5) | data formatting | bytes 77824
  (2 shorter events, 0.0 us)

commit v3 on v2

--- a/solution.py
+++ b/solution.py
@@ -14,7 +14,8 @@
 PAIRS, SLOTS, DEVICES, PIX = 12, 16, 128, 1024
 N_TILE = 16
 EVEN, ODD = 160, 144
-KP = SLOTS * DEVICES
+KP = PAIRS * DEVICES
+GROUP = PAIRS * N_TILE
 OWN = 40
 N_PAIR = 8
 F0_AT, F1_AT, D1_AT, ROWS = 384, 416, 448, 512
@@ -64,30 +65,49 @@
     (ah, al), (bh, bl) = a, b
     return nn(ah, bh) + (nn(ah, bl) + nn(al, bh))
 
-def newton(mats, floors, steps):
-    xs, lows, parts, eyes = [], [], [], []
+def p3(a, b):
+    return product3(split2(a), split2(b))
+
+def p3t(a, b):
+    (ah, al), (bh, bl) = split2(a), split2(b)
+    return nt(ah, bh) + (nt(ah, bl) + nt(al, bh))
+
+def newton_start(mats, floors):
+    xs, lows = [], []
     for m, floor in zip(mats, floors):
         n = m.shape[0]
         top = jnp.max(jnp.sum(jnp.abs(m), axis=1, keepdims=True), axis=0, keepdims=True)
+        c = 2.0 / (top + floor)
+        low = c * floor
+        ab = low * (2.0 - low)
+        k = 2.0 / (1.0 + ab)
         diagonal = iota((n, n), 0) == iota((n, n), 1)
-        xs.append(jnp.where(diagonal, 2.0 / (top + floor), 0.0))
-        lows.append(2.0 * floor / (top + floor))
-        parts.append(split2(m))
-        eyes.append(jnp.where(diagonal, 2.0, 0.0))
+        xs.append((jnp.where(diagonal, 2.0, 0.0) - m * c) * (c * k))
+        lows.append(ab * k)
+    return xs, lows
+
+def newton_steps(mats, state, steps):
+    parts = [split2(m) for m in mats]
     def body(_, carry):
         xs, lows = carry
         nx, nl = [], []
         halves = [split2(x) for x in xs]
         ys = [product3(m, x) for m, x in zip(parts, halves)]
-        for x, y, eye, low in zip(halves, ys, eyes, lows):
+        for x, y, low in zip(halves, ys, lows):
+            n = y.shape[0]
             ab = low * (2.0 - low)
             k = 2.0 / (1.0 + ab)
+            eye = jnp.where(iota((n, n), 0) == iota((n, n), 1), 2.0, 0.0)
             nx.append(product3(x, split2(eye - y)) * k)
             nl.append(ab * k)
         return nx, nl
-    xs, lows = lax.fori_loop(0, steps, body, (xs, lows))
+    return lax.fori_loop(0, steps, body, state)
+
+def newton_end(mats, state):
     out = []
-    for m, x, eye in zip(mats, xs, eyes):
+    for m, x in zip(mats, state[0]):
+        n = m.shape[0]
+        eye = jnp.where(iota((n, n), 0) == iota((n, n), 1), 2.0, 0.0)
         out.append(nn(x, eye - nn(m, x, HI), HI))
     return out
 
@@ -96,9 +116,11 @@
     return jnp.where((pair * 38 + row == date_of(col)) & (row < 38), 1.0, 0.0)
 
 def incidence_rows(pd):
+    unit = jnp.where(iota((8, 2), 0) == iota((8, 2), 1), 1.0, 0.0)
+    row = nt(unit, pd.astype(F32), HI).astype(jnp.int32)
     t = date_of(iota((DATES, KP), 0))
-    later = jnp.where(t == pd[1:2, :], 1.0, 0.0)
-    return later - jnp.where(t == pd[0:1, :], 1.0, 0.0)
+    later = jnp.where(t == row[1:2, :], 1.0, 0.0)
+    return later - jnp.where(t == row[0:1, :], 1.0, 0.0)
 
 def design_rows(at16):
     tt = date_of(iota((DATES, NB), 0)).astype(F32) * ((NB - 3.0) / (DATES - 1.0))
@@ -133,14 +155,24 @@
     return firsts, links, schurs, fits
 
 def full_inverse(first, link, last):
-    right = nn(link, last, HI)
-    top = jnp.concatenate([first + nt(right, link, HI), -right], axis=1)
+    right = p3(link, last)
+    top = jnp.concatenate([first + p3t(right, link), -right], axis=1)
     bottom = jnp.concatenate([-right.T, last], axis=1)
     return jnp.concatenate([top, bottom], axis=0)
 
 def date_solve(inverse, at16, wi):
     hi, lo = split2(inverse)
     return ((nn(hi, at16) + nn(lo, at16)) * wi).astype(BF16)
+
+def spread_own(pair):
+    row, col = iota((KP, SCREEN), 0), iota((KP, SCREEN), 1)
+    inside = (col & 15) < PAIRS
+    return jnp.where((row == GROUP * pair + PAIRS * (col >> 4) + (col & 15)) & inside, 1.0, 0.0).astype(BF16)
+
+def squeeze():
+    row, col = iota((SCREEN, SCREEN), 0), iota((SCREEN, SCREEN), 1)
+    inside = (row & 15) < PAIRS
+    return jnp.where((col == PAIRS * (row >> 4) + (row & 15)) & inside, 1.0, 0.0).astype(BF16)
 
 def knot_rows(code, centers):
     scale = (KNOTS - 3.0) / FRAME
@@ -184,8 +216,12 @@
     def c_copy(other, slot):
         return to_pair(cg.at[pair], cg, c_send, c_recv, other, slot)
 
-    def y_copy(other, slot):
-        return to_tile(sb.at[other], rb, y_send, y_recv, other, slot)
+    def y_copy(other, slot, part):
+        return pltpu.make_async_remote_copy(
+            src_ref=sb.at[other, part], dst_ref=rb.at[slot, part],
+            send_sem=y_send.at[other, part], recv_sem=y_recv.at[slot, part],
+            device_id=(pair, other), device_id_type=MESH,
+        )
 
     def gs_copy(other, slot):
         return to_tile(gs.at[other], gr, gs_send, gs_recv, other, slot)
@@ -224,7 +260,8 @@
         barrier, inc=1, device_id=(pair_peer(i), tile), device_id_type=MESH))
     pl.semaphore_wait(barrier, N_TILE + N_PAIR - 2)
 
-    cg[pair] = ck_ref[...]
+    code = ck_ref[0:1, :] * 65536 + ck_ref[1:2, :]
+    cg[pair] = jnp.concatenate([code[:, i * 128:(i + 1) * 128] for i in range(PIX // 128)], axis=0)
     start_pair(c_copy)
 
     def pack(other, dst):
@@ -242,9 +279,10 @@
     def y_start(i):
         other = tile_peer(i)
         pack(other, sb.at[other])
-        y_copy(other, tile).start()
 
     loop(1, N_TILE, y_start)
+    for part in range(6):
+        loop(1, N_TILE, lambda i, part=part: y_copy(tile_peer(i), tile, part).start())
     pack(tile, rb.at[tile])
 
     wait_pair(c_copy)
@@ -275,21 +313,14 @@
     xt = design_rows(at16)
     firsts, links, schurs, fits = normal_parts(at, at16, xt, w)
 
-    wait_tile(gs_copy)
-    gsum = gr[0]
-    for t in range(1, N_TILE):
-        gsum = gsum + gr[t]
-    gg[tile] = gsum
-    start_tile(gg_copy)
-    wait_tile(gg_copy)
-    gram = gg[...].reshape(SCREEN, SCREEN)
-    gram = gram + jnp.where(iota((SCREEN, SCREEN), 0) == iota((SCREEN, SCREEN), 1), 1.0, 0.0)
-    h, last0, last1, f0, f1 = newton([gram] + schurs + fits, [1.0, 1.0, 1.0, 0.5, 0.5], 11)
+    lasts = newton_start(schurs + fits, [1.0, 1.0, 0.5, 0.5])
+    lasts = newton_steps(schurs + fits, lasts, 8)
+    last0, last1, f0, f1 = newton_end(schurs + fits, lasts)
     sel = own_dates(pair)
-    fit0 = nn(f0, xt * w[0:1, :], HI).astype(BF16)
-    fit1 = nn(f1, xt * w[1:2, :], HI).astype(BF16)
+    fit0 = (p3(f0, xt) * w[0:1, :]).astype(BF16)
+    fit1 = (p3(f1, xt) * w[1:2, :]).astype(BF16)
     d0 = date_solve(full_inverse(firsts[0], links[0], last0), at16, w[0:1, :])
-    d1 = date_solve(nn(sel, full_inverse(firsts[1], links[1], last1), HI), at16, w[1:2, :])
+    d1 = date_solve(p3(sel, full_inverse(firsts[1], links[1], last1)), at16, w[1:2, :])
     lhs[0:DATES] = d0
     lhs[DATES:F0_AT] = jnp.zeros((F0_AT - DATES, KP), BF16)
     lhs[F0_AT:D1_AT] = jnp.concatenate([fit0, fit1], axis=0)
@@ -297,8 +328,15 @@
     xhi, xlo = split2(xt)
     c0 = nt(d0, xhi) + nt(d0, xlo)
     c1 = nt(d1, xhi) + nt(d1, xlo)
-    fa1 = nt(fit1, at16)
-    da1 = nt(d1, at16)
+    ends = jnp.concatenate([nt(fit1, at16), nt(d1, at16), sel], axis=0)
+    fit_own = nn(fit1, spread_own(pair)).astype(BF16)
+
+    wait_tile(gs_copy)
+    gsum = gr[0]
+    for t in range(1, N_TILE):
+        gsum = gsum + gr[t]
+    gg[tile] = gsum
+    start_tile(gg_copy)
 
     def unpack(t):
         rest = [rb[t, 4 + a].astype(F32) for a in range(2)]
@@ -315,12 +353,11 @@
 
     def y_arrive(i):
         other = tile_peer(i)
-        y_copy(other, other).wait_recv()
+        for part in range(6):
+            y_copy(other, other, part).wait_recv()
         unpack(other)
 
     loop(1, N_TILE, y_arrive)
-    fit_own = lhs[F1_AT:D1_AT, pl.ds(pl.multiple_of(pair * SCREEN, SCREEN), SCREEN)]
-
     def z_body(p, acc):
         y = ybuf[p]
         cp[p] = nn(fit_own, y)
@@ -332,40 +369,50 @@
     start_pair(f_copy)
     zr[tile] = zs[tile]
     cr[pair] = cp[pair]
+    wait_tile(gg_copy)
+    gram = gg[...].reshape(SCREEN, SCREEN)
+    gram = gram + jnp.where(iota((SCREEN, SCREEN), 0) == iota((SCREEN, SCREEN), 1), 1.0, 0.0)
+    state = newton_start([gram], [1.0])
+    state = newton_steps([gram], state, 3)
     wait_tile(zs_copy)
     zsum = zr[0]
     for t in range(1, N_TILE):
         zsum = zsum + zr[t]
-    zg[pair] = zsum
+    zhi, zlo = split2(zsum)
+    zg[pair] = nn(jnp.concatenate([zhi, zlo], axis=0), squeeze()).astype(BF16)
     start_pair(zg_copy)
+    state = newton_steps([gram], state, 3)
     wait_pair(zg_copy)
-    zrow = jnp.concatenate([zg[p] for p in range(N_PAIR)], axis=1)
-    zhi, zlo = split2(zrow)
-    both = nt(jnp.concatenate([zhi, zlo], axis=0), lhs[...])
+    zrow = jnp.concatenate([zg[p].astype(F32)[:, 0:GROUP] for p in range(N_PAIR)], axis=1).astype(BF16)
+    both = nt(zrow, lhs[...])
     wg[tile] = both[0:KNOTS] + both[KNOTS:2 * KNOTS]
     start_tile(w_copy)
-    wait_tile(w_copy)
-
-    wt = wg[...].reshape(SCREEN, ROWS)
-    w0 = wt[:, 0:DATES] - nt(wt[:, F0_AT:F1_AT], c0, HI)
-    s1 = nn(h, w0, HI)
-    e = nt(s1, fa1, HI).T
-    v = w0 - s1
-    fz1 = wt[:, F1_AT:D1_AT] - nt(v, fa1, HI)
-    dz1 = wt[:, D1_AT:D1_AT + OWN] - nt(v, da1, HI)
-    s2 = nt(s1, sel, HI) + nn(h, dz1 - nt(fz1, c1, HI), HI)
-    sc_ref[...] = s2.T[0:38]
+    state = newton_steps([gram], state, 3)
+    (h,) = newton_end([gram], state)
     wait_pair(f_copy)
-    ehi, elo = split2(e)
-    own_knots = bhi[pair]
     total = cr[0]
     for p in range(1, N_PAIR):
         total = total + cr[p]
+    wait_tile(w_copy)
+
+    wt = wg[...].reshape(SCREEN, ROWS)
+    w0 = wt[:, 0:DATES] - p3t(wt[:, F0_AT:F1_AT], c0)
+    s1 = p3(h, w0)
+    q0 = p3t(w0, ends[0:NB + OWN])
+    q1 = p3t(s1, ends)
+    ehi, elo = split2(q1[:, 0:NB].T)
+    own_knots = bhi[pair]
     co_ref[...] = total - (nn(ehi, own_knots) + nn(elo, own_knots))
+    step = wt[:, F1_AT:D1_AT + OWN] - (q0 - q1[:, 0:NB + OWN])
+    change = step[:, NB:] - p3t(step[:, 0:NB], c1)
+    s2 = q1[:, NB + OWN:] + p3(h, change)
+    sc_ref[...] = s2.T[0:38]
 
     def drain_tile(i):
         other = tile_peer(i)
-        for copy in (y_copy, gs_copy, gg_copy, zs_copy, w_copy):
+        for part in range(6):
+            y_copy(other, tile, part).wait_send()
+        for copy in (gs_copy, gg_copy, zs_copy, w_copy):
             copy(other, tile).wait_send()
 
     loop(1, N_TILE, drain_tile)
@@ -379,14 +426,10 @@
 
 
 def local(phases, pair_dates, weights, coords):
-    pd = jnp.pad(pair_dates.reshape(DEVICES, PAIRS, 2), ((0, 0), (0, SLOTS - PAIRS), (0, 0)), constant_values=-1)
-    pd = pd.reshape(KP, 2).T
-    w = jnp.pad(weights.reshape(2, DEVICES, PAIRS), ((0, 0), (0, 0), (0, SLOTS - PAIRS))).reshape(2, KP)
-    codes = (coords[0] * 65536 + coords[1]).reshape(PIX // 128, 128)
     vmem = pl.BlockSpec(memory_space=pltpu.VMEM)
     shape = jax.ShapeDtypeStruct
     dma = pltpu.SemaphoreType.DMA
-    tiles, pairs = dma((N_TILE,)), dma((N_PAIR,))
+    tiles, pairs, parts = dma((N_TILE,)), dma((N_PAIR,)), dma((N_TILE, 6))
     return pl.pallas_call(
         mega_kernel,
         out_shape=[shape((NB, PIX), F32), shape((38, SCREEN), F32)],
@@ -404,19 +447,19 @@
             pltpu.VMEM((N_TILE, KNOTS, SCREEN), F32),
             pltpu.VMEM((N_TILE, KNOTS, SCREEN), F32),
             pltpu.VMEM((N_TILE, KNOTS, SCREEN), F32),
-            pltpu.VMEM((N_PAIR, KNOTS, SCREEN), F32),
+            pltpu.VMEM((N_PAIR, 2 * KNOTS, SCREEN), BF16),
             pltpu.VMEM((N_TILE, KNOTS, ROWS), F32),
             pltpu.VMEM((N_PAIR, NB, PIX), F32),
             pltpu.VMEM((N_PAIR, NB, PIX), F32),
             pltpu.VMEM((ROWS, KP), BF16),
-            pairs, pairs, tiles, tiles, tiles, tiles, tiles, tiles,
+            pairs, pairs, parts, parts, tiles, tiles, tiles, tiles,
             tiles, tiles, pairs, pairs, tiles, tiles, pairs, pairs,
         ],
         compiler_params=pltpu.CompilerParams(
             collective_id=0, has_side_effects=True, vmem_limit_bytes=VMEM_LIMIT
         ),
         name="mega",
-    )(phases, codes, pd, w)
+    )(phases, coords, pair_dates, weights)
 
 
 def solution(mesh):

time: 134 us -> 96.2 us (0.72)
  Pallas kernels: 125 us -> 90.4 us
  other arithmetic: 1.36 us -> 0 us
    pallas_call x1, Pallas kernels: 125 us -> 90.4 us  [local(): pl.pallas_call(mega_kernel, out_shape=[shape((NB, PIX), F32), shape((38,...]
    reshape x4 -> x0, local copies, waits for them, and re-layouts: 3.15 us -> none  [the longest x1 0.85 us: local(): weights.reshape(2, DEVICES, PAIRS)]
    unnamed x2 -> x3, local copies, waits for them, and re-layouts: 2.97 us -> 4.86 us
    add x1 -> x0, other arithmetic: 1.36 us -> none  [local(): codes = (coords[0] * 65536 + coords[1]).reshape(PIX // 128, 128)]
where the time goes in v3:
time: 96.2 us; the launch traced here: 95.9 us
  Pallas kernels  90.4 us (94%)
  local copies, waits for them, and re-layouts  4.86 us (5%)
    pallas_call x1, Pallas kernels, local(): pl.pallas_call(mega_kernel, out_shape=[shape((NB, PIX), F32), shape((38,...  90.4 us
    unnamed x3, local copies, waits for them, and re-layouts  4.86 us

profile of v3, /device:TPU:1, one launch (start us, length us, event | category | flops | bytes accessed | tf_op | source)
XLA Modules:
  0.0 95.9 jit_solution(17404954234809216019)
XLA Ops:
  0.6 1.9 %copy.6.pd_ref = s32[1536,2]{1,0:T(8,128)} copy(s32[1536,2]{0,1:T(2,128)} %param.5) | data formatting | bytes 24576 | tf_op args[1]
  2.5 90.4 %mega.1 = (f32[32,1024]{1,0:T(8,128)}, f32[38,256]{1,0:T(8,128)}) custom-call(bf16[12,131072]{1,0:T(8,128)(2,1)} %ph_ref.1, s32[2,1024]{1,0:T(2,128)} %ck_ref.1, s32[1536,2]{1,0:T(8,128)} %copy.6.pd_ref, f32[2,1536]{1,0:T(2,128)} %w_ref.1), custom_call_target="tpu_custom_call" | custom-call | tf_op jit(solution)/shard_map/mega/pallas_call | solution.py:433
  93.0 1.6 %copy.9 = f32[32,1024]{1,0:T(8,128)} copy(f32[32,1024]{1,0:T(8,128)} %get-tuple-element.4) | data formatting | bytes 262144
  94.5 1.4 %copy.10 = f32[38,256]{1,0:T(8,128)} copy(f32[38,256]{1,0:T(8,128)} %get-tuple-element.5) | data formatting | bytes 77824

commit v4 on v3

v4 whole, which is shorter than its diff:
```python
import functools

import jax
import jax.numpy as jnp
from jax import lax
from jax.experimental import pallas as pl
from jax.experimental.pallas import tpu as pltpu
from jax.sharding import PartitionSpec as P

MESH = pl.DeviceIdType.MESH
HI = lax.Precision.HIGHEST
F32, BF16 = jnp.float32, jnp.bfloat16
DATES, NB, KNOTS, FRAME, SCREEN = 304, 32, 16, 4096, 256
PAIRS, SLOTS, DEVICES, PIX = 12, 16, 128, 1024
NPIX = DEVICES * PIX
N_TILE = 16
EVEN, ODD = 160, 144
KP = PAIRS * DEVICES
GROUP = PAIRS * N_TILE
OWN = 40
N_PAIR = 8
NEAR = 160
F0_AT, F1_AT, D1_AT, ROWS = 384, 416, 448, 608
HALF = PIX // 2
PARTS = 1
VMEM_LIMIT = 60 * 1024 * 1024

def nn(a, b, precision=None):
    return lax.dot_general(a, b, (((1,), (0,)), ((), ())), precision=precision, preferred_element_type=F32)

def nt(a, b, precision=None):
    return lax.dot_general(a, b, (((1,), (1,)), ((), ())), precision=precision, preferred_element_type=F32)

def tn(a, b, precision=None):
    return lax.dot_general(a, b, (((0,), (0,)), ((), ())), precision=precision, preferred_element_type=F32)

def split2(x):
    hi = x.astype(BF16)
    return hi, (x - hi.astype(F32)).astype(BF16)

def spline(s):
    a = jnp.abs(s)
    r = jnp.maximum(2.0 - a, 0.0)
    q = jnp.maximum(1.0 - a, 0.0)
    return (r * r * r - 4.0 * (q * q * q)) * (1.0 / 6.0)

def date_of(r):
    rr = jnp.where(r < EVEN, r, r - EVEN)
    base = ((rr >> 4) << 5) + (rr & 15)
    return jnp.where(r < EVEN, base, base + 16)

def iota(shape, dim):
    return lax.broadcasted_iota(jnp.int32, shape, dim)

def block_inverse(c):
    n = c.shape[1]
    row = iota((1, n, n), 1)
    col = iota((1, n, n), 2)
    for j in range(n):
        prow = c[:, j:j + 1, :]
        pcol = c[:, :, j:j + 1]
        d = 1.0 / c[:, j:j + 1, j:j + 1]
        newrow = jnp.where(col[:, :1, :] == j, 1.0, prow) * d
        base = jnp.where(col == j, 0.0, c)
        c = jnp.where(row == j, newrow, base - pcol * newrow)
    return c

def product3(a, b):
    (ah, al), (bh, bl) = a, b
    return nn(ah, bh) + (nn(ah, bl) + nn(al, bh))

def p3(a, b):
    return product3(split2(a), split2(b))

def p3t(a, b):
    (ah, al), (bh, bl) = split2(a), split2(b)
    return nt(ah, bh) + (nt(ah, bl) + nt(al, bh))

def newton_start(mats, floors):
    xs, lows = [], []
    for m, floor in zip(mats, floors):
        n = m.shape[0]
        top = jnp.max(jnp.sum(jnp.abs(m), axis=1, keepdims=True), axis=0, keepdims=True)
        c = 2.0 / (top + floor)
        low = c * floor
        ab = low * (2.0 - low)
        k = 2.0 / (1.0 + ab)
        diagonal = iota((n, n), 0) == iota((n, n), 1)
        xs.append((jnp.where(diagonal, 2.0, 0.0) - m * c) * (c * k))
        lows.append(ab * k)
    return xs, lows

def newton_steps(mats, state, steps):
    parts = [split2(m) for m in mats]
    def body(_, carry):
        xs, lows = carry
        nx, nl = [], []
        halves = [split2(x) for x in xs]
        ys = [product3(m, x) for m, x in zip(parts, halves)]
        for x, y, low in zip(halves, ys, lows):
            n = y.shape[0]
            ab = low * (2.0 - low)
            k = 2.0 / (1.0 + ab)
            eye = jnp.where(iota((n, n), 0) == iota((n, n), 1), 2.0, 0.0)
            nx.append(product3(x, split2(eye - y)) * k)
            nl.append(ab * k)
        return nx, nl
    return lax.fori_loop(0, steps, body, state)

def newton_end(mats, state):
    out = []
    for m, x in zip(mats, state[0]):
        n = m.shape[0]
        eye = jnp.where(iota((n, n), 0) == iota((n, n), 1), 2.0, 0.0)
        out.append(nn(x, eye - nn(m, x, HI), HI))
    return out

def near_dates(quarter):
    row, col = iota((NEAR, DATES), 0), iota((NEAR, DATES), 1)
    q = jnp.where(row >= 2 * OWN, jnp.where(row >= 3 * OWN, 3, 2), jnp.where(row >= OWN, 1, 0))
    i = row - OWN * q
    return jnp.where((38 * (4 * quarter + q) + i == date_of(col)) & (i < 38), 1.0, 0.0)

def by_group(x):
    lane = iota((8, KP), 1)
    t = (lane * 21846) >> 18
    delta = ((t >> 4) & 3) - ((t >> 2) & 3)
    out = x
    for d in (-3, -2, -1, 1, 2, 3):
        out = jnp.where(delta == d, pltpu.roll(x, (144 * d) % KP, 1), out)
    return out

def incidence_rows(pd):
    t = date_of(iota((DATES, KP), 0))
    later = jnp.where(t == pd[1:2, :], 1.0, 0.0)
    return later - jnp.where(t == pd[0:1, :], 1.0, 0.0)

def design_rows(at16):
    tt = date_of(iota((DATES, NB), 0)).astype(F32) * ((NB - 3.0) / (DATES - 1.0))
    t1 = spline(tt - (iota((DATES, NB), 1).astype(F32) - 1.0)).T
    a = t1.astype(BF16)
    r = t1 - a.astype(F32)
    b, c = split2(r)
    return nn(a, at16) + nn(b, at16) + nn(c, at16)

def normal_parts(at, at16, xt, w):
    eye = jnp.where(iota((DATES, DATES), 0) == iota((DATES, DATES), 1), 1.0, 0.0)
    fold = jnp.where((iota((EVEN, 16), 0) & 15) == iota((EVEN, 16), 1), 1.0, 0.0)
    mask = (iota((EVEN, EVEN), 0) >> 4) == (iota((EVEN, EVEN), 1) >> 4)
    ns, comps, fits = [], [], []
    for i in range(2):
        wi = w[i:i + 1, :]
        hi, lo = split2(wi)
        n = nt((at * hi.astype(F32)).astype(BF16), at16) + nt((at * lo.astype(F32)).astype(BF16), at16) + eye
        ns.append(n)
        comps.append(nn(jnp.where(mask, n[:EVEN, :EVEN], 0.0), fold, HI).reshape(10, 16, 16))
        fits.append(nt(xt * wi, xt, HI) + jnp.where(iota((NB, NB), 0) == iota((NB, NB), 1), 0.5, 0.0))
    inv = block_inverse(jnp.concatenate(comps, axis=0))
    firsts, links, schurs = [], [], []
    for i in range(2):
        compact = inv[10 * i:10 * i + 10].reshape(EVEN, 16)
        first = jnp.where(mask, nt(compact, fold, HI), 0.0)
        e = ns[i][:EVEN, EVEN:]
        y = nn(first, e, HI)
        schurs.append(ns[i][EVEN:, EVEN:] - tn(e, y, HI))
        firsts.append(first)
        links.append(y)
    return firsts, links, schurs, fits

def full_inverse(first, link, last):
    right = p3(link, last)
    top = jnp.concatenate([first + p3t(right, link), -right], axis=1)
    bottom = jnp.concatenate([-right.T, last], axis=1)
    return jnp.concatenate([top, bottom], axis=0)

def date_solve(inverse, at16, wi):
    hi, lo = split2(inverse)
    return ((nn(hi, at16) + nn(lo, at16)) * wi).astype(BF16)

def spread_own(group_of_residue):
    row, col = iota((KP, SCREEN), 0), iota((KP, SCREEN), 1)
    group = group_of_residue(iota((1, SCREEN), 1) >> 4)
    inside = (col & 15) < PAIRS
    return jnp.where((row == GROUP * group + PAIRS * (col >> 4) + (col & 15)) & inside, 1.0, 0.0).astype(BF16)

def squeeze():
    row, col = iota((SCREEN, SCREEN), 0), iota((SCREEN, SCREEN), 1)
    inside = (row & 15) < PAIRS
    return jnp.where((col == PAIRS * (row >> 4) + (row & 15)) & inside, 1.0, 0.0).astype(BF16)

def knot_rows(code, centers):
    scale = (KNOTS - 3.0) / FRAME
    rows = spline((code >> 16).astype(F32) * scale - centers)
    cols = spline((code & 65535).astype(F32) * scale - centers)
    return rows, cols


def mega_kernel(
    ph_hbm, ck_ref, pd_ref, w_ref, co_ref, sc_ref,
    ph_ref, ph_sem, cg, sb, rb, bhi, blo_ref, ybuf, gs, gr, gg, zs, zr, zg, wq, wg, cp, cr, lhs,
    c_send, c_recv, y_send, y_recv, gs_send, gs_recv, gg_send, gg_recv,
    zs_send, zs_recv, zg_send, zg_recv, w_send, w_recv, f_send, f_recv,
):
    pair, tile = lax.axis_index("pair"), lax.axis_index("tile")
    zh, zl, yl = pair // 4, (pair // 2) % 2, pair % 2
    yh, xh, xl, core = tile // 8, (tile // 4) % 2, (tile // 2) % 2, tile % 2
    me = zl * 8 + yl * 4 + xl * 2 + core
    group = zh * 4 + yh * 2 + xh

    def place(a, r):
        p = (a // 4) * 4 + (r // 8) * 2 + (r // 4) % 2
        return p, ((a // 2) % 2) * 8 + (a % 2) * 4 + r % 4

    def group_at(r, half):
        if half == 0:
            return group
        return (
            ((zh + zl + r // 8) % 2) * 4 + ((yh + yl + (r // 4) % 2) % 2) * 2 + (xh + xl + (r // 2) % 2) % 2
        )

    def residue_peer(i):
        t = me + i
        return jnp.where(t >= N_TILE, t - N_TILE, t)

    def class_peer(i):
        t = group + i
        return jnp.where(t >= N_PAIR, t - N_PAIR, t)

    def loop(lo, hi, f):
        def body(i, carry):
            f(i)
            return carry
        lax.fori_loop(lo, hi, body, 0)

    def to_residue(src, dst, send, recv, other, half=0):
        return pltpu.make_async_remote_copy(
            src_ref=src, dst_ref=dst, send_sem=send, recv_sem=recv,
            device_id=place(group_at(other, half), other), device_id_type=MESH,
        )

    def to_class(src, dst, send, recv, other, slot):
        return pltpu.make_async_remote_copy(
            src_ref=src, dst_ref=dst.at[slot], send_sem=send.at[other], recv_sem=recv.at[slot],
            device_id=place(other, me), device_id_type=MESH,
        )

    def c_copy(other, slot):
        return to_class(cg.at[group], cg, c_send, c_recv, other, slot)

    def y_copy(other, slot, half, part):
        rows = pl.ds(6 * part, 6)
        return to_residue(
            sb.at[half, other, rows], rb.at[half, slot, rows],
            y_send.at[half, other, part], y_recv.at[half, slot, part], other, half,
        )

    def gs_copy(other, slot):
        return to_residue(gs.at[other], gr.at[slot], gs_send.at[other], gs_recv.at[slot], other)

    def gg_copy(other, slot):
        return to_residue(gg.at[me], gg.at[slot], gg_send.at[other], gg_recv.at[slot], other)

    def zs_copy(other, slot, half):
        return to_residue(
            zs.at[half, other], zr.at[half, slot], zs_send.at[half, other], zs_recv.at[half, slot], other, half
        )

    def zg_copy(other, slot):
        return to_class(zg.at[group], zg, zg_send, zg_recv, other, slot)

    def w_copy(other, slot):
        return to_residue(wq.at[other // 4], wg.at[slot], w_send.at[other], w_recv.at[slot], other)

    def f_copy(other, slot, half):
        return to_class(cp.at[half, other], cr.at[half], f_send.at[half], f_recv.at[half], other, slot)

    def start_residue(copy, *more):
        loop(1, N_TILE, lambda i: copy(residue_peer(i), me, *more).start())

    def wait_residue(copy, *more):
        loop(1, N_TILE, lambda i: copy(residue_peer(i), residue_peer(i), *more).wait_recv())

    def start_class(copy, *more):
        loop(1, N_PAIR, lambda i: copy(class_peer(i), group, *more).start())

    def wait_class(copy, *more):
        loop(1, N_PAIR, lambda i: copy(class_peer(i), class_peer(i), *more).wait_recv())

    load = pltpu.make_async_copy(ph_hbm, ph_ref, ph_sem)
    load.start()
    barrier = pltpu.get_barrier_semaphore()

    def greet(where):
        pl.semaphore_signal(barrier, inc=1, device_id=where, device_id_type=MESH)

    for half in range(2):
        loop(1, N_TILE, lambda i, half=half: greet(place(group_at(residue_peer(i), half), residue_peer(i))))
    loop(1, N_PAIR, lambda i: greet(place(class_peer(i), me)))

    rows = jnp.concatenate([pd_ref[...].astype(F32), w_ref[...], jnp.zeros((4, KP), F32)], axis=0)
    rows = by_group(rows)
    w = rows[2:4, :]
    at = incidence_rows(rows[0:2, :].astype(jnp.int32))
    at16 = at.astype(BF16)
    xt = design_rows(at16)
    firsts, links, schurs, fits = normal_parts(at, at16, xt, w)
    pl.semaphore_wait(barrier, 2 * N_TILE + N_PAIR - 3)

    code = ck_ref[0:1, :] * 65536 + ck_ref[1:2, :]
    cg[group] = jnp.concatenate([code[:, i * 128:(i + 1) * 128] for i in range(PIX // 128)], axis=0)
    start_class(c_copy)

    load.wait()

    def pack(other, half, dst):
        blocks = []
        for a in range(N_PAIR):
            p, t = place(a, other)
            first = pl.multiple_of((p * N_TILE + t) * PIX + half * HALF, HALF)
            blocks.append(ph_ref[:, pl.ds(first, HALF)].astype(F32))
        for a in range(4):
            two = jnp.concatenate([blocks[2 * a][0:8], blocks[2 * a + 1][0:8]], axis=0)
            dst[a] = two.astype(BF16)
        for a in range(2):
            four = jnp.concatenate([blocks[4 * a + q][8:12] for q in range(4)], axis=0)
            dst[4 + a] = four.astype(BF16)

    def y_start(i, half):
        other = residue_peer(i)
        pack(other, half, sb.at[half, other])
        for part in range(PARTS):
            y_copy(other, me, half, part).start()

    for half in range(2):
        loop(1, N_TILE, lambda i, half=half: y_start(i, half))
    for half in range(2):
        pack(me, half, rb.at[half, me])

    lasts = newton_start(schurs + fits, [1.0, 1.0, 0.5, 0.5])
    lasts = newton_steps(schurs + fits, lasts, 8)
    last0, last1, f0, f1 = newton_end(schurs + fits, lasts)

    wait_class(c_copy)
    centers = iota((KNOTS, 1), 0).astype(F32) - 1.0

    def knots(p, carry):
        g1, g2 = carry
        for i in range(PIX // 128):
            rows, cols = knot_rows(cg[p, i:i + 1, :], centers)
            lanes = pl.ds(i * 128, 128)
            for m in range(KNOTS):
                hi, lo = split2(rows[m:m + 1, :] * cols)
                bhi[p, m * KNOTS:(m + 1) * KNOTS, lanes] = hi
                blo_ref[m * KNOTS:(m + 1) * KNOTS, lanes] = lo
        hi = bhi[p]
        return g1 + nt(hi, hi), g2 + nt(hi, blo_ref[...])

    zero = jnp.zeros((SCREEN, SCREEN), F32)
    g1, g2 = lax.fori_loop(0, N_PAIR, knots, (zero, zero))
    gs[...] = (g1 + g2 + g2.T).reshape(N_TILE, KNOTS, SCREEN)
    start_residue(gs_copy)
    gr[me] = gs[me]

    sel = near_dates(zh)
    fit0 = (p3(f0, xt) * w[0:1, :]).astype(BF16)
    fit1 = (p3(f1, xt) * w[1:2, :]).astype(BF16)
    d0 = date_solve(full_inverse(firsts[0], links[0], last0), at16, w[0:1, :])
    d1 = date_solve(p3(sel, full_inverse(firsts[1], links[1], last1)), at16, w[1:2, :])
    lhs[0:DATES] = d0
    lhs[DATES:F0_AT] = jnp.zeros((F0_AT - DATES, KP), BF16)
    lhs[F0_AT:D1_AT] = jnp.concatenate([fit0, fit1], axis=0)
    lhs[D1_AT:ROWS] = d1
    xhi, xlo = split2(xt)
    c0 = nt(d0, xhi) + nt(d0, xlo)
    c1 = nt(d1, xhi) + nt(d1, xlo)
    ends = jnp.concatenate([nt(fit1, at16), nt(d1, at16), sel], axis=0)
    fit_own = [nn(fit1, spread_own(functools.partial(group_at, half=half))).astype(BF16) for half in range(2)]

    wait_residue(gs_copy)
    gsum = gr[0]
    for t in range(1, N_TILE):
        gsum = gsum + gr[t]
    gg[me] = gsum
    start_residue(gg_copy)

    def unpack(t, half):
        rest = [rb[half, t, 4 + a].astype(F32) for a in range(2)]
        for a in range(4):
            two = rb[half, t, a].astype(F32)
            for b in range(2):
                p = 2 * a + b
                low = rest[p // 4][4 * (p % 4):4 * (p % 4) + 4]
                block = jnp.concatenate([two[8 * b:8 * b + 8], low, jnp.zeros((4, HALF), F32)], axis=0)
                ybuf[half, p, pl.ds(pl.multiple_of(t * SLOTS, SLOTS), SLOTS), :] = block.astype(BF16)

    def y_arrive(i, half):
        other = residue_peer(i)
        for part in range(PARTS):
            y_copy(other, other, half, part).wait_recv()
        unpack(other, half)

    def z_body(p, acc, half):
        y = ybuf[half, p]
        cp[half, p] = nn(fit_own[half], y).astype(BF16)
        return acc + nt(bhi[p, :, half * HALF:(half + 1) * HALF], y)

    for half in range(2):
        unpack(me, half)
        loop(1, N_TILE, lambda i, half=half: y_arrive(i, half))
        zt = lax.fori_loop(0, N_PAIR, functools.partial(z_body, half=half), zero)
        zs[half] = zt.reshape(N_TILE, KNOTS, SCREEN)
        start_residue(zs_copy, half)
        zr[half, me] = zs[half, me]
        cr[half, group] = cp[half, group]
    wait_residue(gg_copy)
    gram = gg[...].reshape(SCREEN, SCREEN)
    gram = gram + jnp.where(iota((SCREEN, SCREEN), 0) == iota((SCREEN, SCREEN), 1), 1.0, 0.0)
    state = newton_start([gram], [1.0])
    state = newton_steps([gram], state, 3)
    sums = []
    for half in range(2):
        wait_residue(zs_copy, half)
        zsum = zr[half, 0]
        for t in range(1, N_TILE):
            zsum = zsum + zr[half, t]
        sums.extend(split2(zsum))
    zg[group] = nn(jnp.concatenate(sums, axis=0), squeeze()).astype(BF16)
    start_class(zg_copy)
    for half in range(2):
        start_class(f_copy, half)
    state = newton_steps([gram], state, 3)
    wait_class(zg_copy)
    octant = iota((1, SCREEN), 1)
    octant = jnp.where(octant < GROUP, (octant * 10923) >> 18, -1)
    across = []
    for a in range(N_PAIR):
        b = ((zl + a // 4) % 2) * 4 + ((yl + (a // 2) % 2) % 2) * 2 + (xl + a % 2) % 2
        both = zg[b].astype(F32)
        across.append(both[2 * KNOTS:3 * KNOTS] + both[3 * KNOTS:4 * KNOTS])
    zrow = []
    for a in range(N_PAIR):
        both = zg[a].astype(F32)
        here = both[0:KNOTS] + both[KNOTS:2 * KNOTS]
        for m in range(N_PAIR):
            here = here + jnp.where(octant == m, across[a ^ m], 0.0)
        zrow.append(here[:, 0:GROUP])
    zhi, zlo = split2(jnp.concatenate(zrow, axis=1))
    both = nt(jnp.concatenate([zhi, zlo], axis=0), lhs[...])
    wt = both[0:KNOTS] + both[KNOTS:2 * KNOTS]
    w0 = wt[:, 0:DATES] - p3t(wt[:, F0_AT:F1_AT], c0)
    q = p3t(w0, ends)
    for n in range(4):
        lo = n * OWN
        wq[n] = jnp.concatenate([
            q[:, 0:NB], q[:, NB + lo:NB + lo + OWN], q[:, NB + NEAR + lo:NB + NEAR + lo + OWN],
            jnp.zeros((KNOTS, 128 - NB - 2 * OWN), F32),
            wt[:, F1_AT:D1_AT], wt[:, D1_AT + lo:D1_AT + lo + OWN], jnp.zeros((KNOTS, 128 - NB - OWN), F32),
        ], axis=1)
    start_residue(w_copy)
    wg[me] = wq[me // 4]
    state = newton_steps([gram], state, 3)
    (h,) = newton_end([gram], state)
    mine = zl * 2 + yl
    c1_own = c1[0:OWN]
    for n in range(1, 4):
        c1_own = jnp.where(mine == n, c1[n * OWN:(n + 1) * OWN], c1_own)
    totals = []
    for half in range(2):
        wait_class(f_copy, half)
        total = cr[half, 0].astype(F32)
        for p in range(1, N_PAIR):
            total = total + cr[half, p].astype(F32)
        totals.append(total)
    total = jnp.concatenate(totals, axis=1)
    wait_residue(w_copy)

    wt = wg[...].reshape(SCREEN, 2 * 128)
    q0 = wt[:, 0:128]
    q1 = p3(h, q0)
    ehi, elo = split2(q1[:, 0:NB].T)
    own_knots = bhi[group]
    co_ref[...] = total - (nn(ehi, own_knots) + nn(elo, own_knots))
    step = wt[:, 128:128 + NB + OWN] - (q0[:, 0:NB + OWN] - q1[:, 0:NB + OWN])
    change = step[:, NB:] - p3t(step[:, 0:NB], c1_own)
    s2 = q1[:, NB + OWN:NB + 2 * OWN] + p3(h, change)
    sc_ref[...] = s2.T[0:38]

    def drain_residue(i):
        other = residue_peer(i)
        for half in range(2):
            for part in range(PARTS):
                y_copy(other, me, half, part).wait_send()
            zs_copy(other, me, half).wait_send()
        for copy in (gs_copy, gg_copy, w_copy):
            copy(other, me).wait_send()

    loop(1, N_TILE, drain_residue)

    def drain_class(i):
        other = class_peer(i)
        for copy in (c_copy, zg_copy):
            copy(other, group).wait_send()
        for half in range(2):
            f_copy(other, group, half).wait_send()

    loop(1, N_PAIR, drain_class)


def local(phases, pair_dates, weights, coords):
    vmem = pl.BlockSpec(memory_space=pltpu.VMEM)
    shape = jax.ShapeDtypeStruct
    dma = pltpu.SemaphoreType.DMA
    tiles, pairs = dma((N_TILE,)), dma((N_PAIR,))
    twos, halves, parts = dma((2, N_PAIR)), dma((2, N_TILE)), dma((2, N_TILE, PARTS))
    return pl.pallas_call(
        mega_kernel,
        out_shape=[shape((NB, PIX), F32), shape((38, SCREEN), F32)],
        in_specs=[pl.BlockSpec(memory_space=pl.ANY)] + [vmem] * 3,
        out_specs=[vmem] * 2,
        scratch_shapes=[
            pltpu.VMEM((PAIRS, NPIX), BF16),
            dma,
            pltpu.VMEM((N_PAIR, PIX // 128, 128), jnp.int32),
            pltpu.VMEM((2, N_TILE, 6, SLOTS, HALF), BF16),
            pltpu.VMEM((2, N_TILE, 6, SLOTS, HALF), BF16),
            pltpu.VMEM((N_PAIR, SCREEN, PIX), BF16),
            pltpu.VMEM((SCREEN, PIX), BF16),
            pltpu.VMEM((2, N_PAIR, SCREEN, HALF), BF16),
            pltpu.VMEM((N_TILE, KNOTS, SCREEN), F32),
            pltpu.VMEM((N_TILE, KNOTS, SCREEN), F32),
            pltpu.VMEM((N_TILE, KNOTS, SCREEN), F32),
            pltpu.VMEM((2, N_TILE, KNOTS, SCREEN), F32),
            pltpu.VMEM((2, N_TILE, KNOTS, SCREEN), F32),
            pltpu.VMEM((N_PAIR, 4 * KNOTS, SCREEN), BF16),
            pltpu.VMEM((4, KNOTS, 2 * 128), F32),
            pltpu.VMEM((N_TILE, KNOTS, 2 * 128), F32),
            pltpu.VMEM((2, N_PAIR, NB, HALF), BF16),
            pltpu.VMEM((2, N_PAIR, NB, HALF), BF16),
            pltpu.VMEM((ROWS, KP), BF16),
            pairs, pairs, parts, parts, tiles, tiles, tiles, tiles,
            halves, halves, pairs, pairs, tiles, tiles, twos, twos,
        ],
        compiler_params=pltpu.CompilerParams(
            collective_id=0, has_side_effects=True, vmem_limit_bytes=VMEM_LIMIT
        ),
        name="mega",
    )(phases, coords, pair_dates.T, weights)


def solution(mesh):
    return jax.shard_map(
        local,
        mesh=mesh,
        in_specs=(P(("pair", "tile"), None), P(), P(), P(None, ("pair", "tile"))),
        out_specs=(P(None, ("pair", "tile")), P("pair", None)),
        check_vma=False,
    )
```

time: 96.2 us -> 74.7 us (0.78)
  Pallas kernels: 90.4 us -> 70.9 us
  local copies, waits for them, and re-layouts: 4.86 us -> 2.97 us
    pallas_call x1, Pallas kernels: 90.4 us -> 70.9 us  [local(): pl.pallas_call(mega_kernel, out_shape=[shape((NB, PIX), F32), shape((38,...]
    unnamed x3 -> x2, local copies, waits for them, and re-layouts: 4.86 us -> 2.97 us
where the time goes in v4:
time: 74.7 us; the launch traced here: 74.5 us
  Pallas kernels  70.9 us (95%)
  local copies, waits for them, and re-layouts  2.97 us (4%)
    pallas_call x1, Pallas kernels, local(): pl.pallas_call(mega_kernel, out_shape=[shape((NB, PIX), F32), shape((38,...  70.9 us
    unnamed x2, local copies, waits for them, and re-layouts  2.97 us

profile of v4, /device:TPU:1, one launch (start us, length us, event | category | flops | bytes accessed | tf_op | source)
XLA Modules:
  0.0 74.5 jit_solution(330330663513262910)
XLA Ops:
  0.6 70.9 %mega.1 = (f32[32,1024]{1,0:T(8,128)}, f32[38,256]{1,0:T(8,128)}) custom-call(bf16[12,131072]{1,0:T(8,128)(2,1)} %ph_hbm.1, s32[2,1024]{1,0:T(2,128)} %ck_ref.1, s32[2,1536]{1,0:T(2,128)} %bitcast.1, f32[2,1536]{1,0:T(2,128)} %w_ref.1), custom_call_target="tpu_custom_call" | custom-call | tf_op jit(solution)/shard_map/mega/pallas_call | solution.py:515
  71.5 1.6 %copy.8 = f32[32,1024]{1,0:T(8,128)} copy(f32[32,1024]{1,0:T(8,128)} %get-tuple-element.4) | data formatting | bytes 262144
  73.1 1.4 %copy.9 = f32[38,256]{1,0:T(8,128)} copy(f32[38,256]{1,0:T(8,128)} %get-tuple-element.5) | data formatting | bytes 77824

commit v5 on v4

--- a/solution.py
+++ b/solution.py
@@ -155,6 +155,11 @@
         ns.append(n)
         comps.append(nn(jnp.where(mask, n[:EVEN, :EVEN], 0.0), fold, HI).reshape(10, 16, 16))
         fits.append(nt(xt * wi, xt, HI) + jnp.where(iota((NB, NB), 0) == iota((NB, NB), 1), 0.5, 0.0))
+    return ns, comps, fits
+
+def eliminate_even(ns, comps):
+    fold = jnp.where((iota((EVEN, 16), 0) & 15) == iota((EVEN, 16), 1), 1.0, 0.0)
+    mask = (iota((EVEN, EVEN), 0) >> 4) == (iota((EVEN, EVEN), 1) >> 4)
     inv = block_inverse(jnp.concatenate(comps, axis=0))
     firsts, links, schurs = [], [], []
     for i in range(2):
@@ -165,7 +170,7 @@
         schurs.append(ns[i][EVEN:, EVEN:] - tn(e, y, HI))
         firsts.append(first)
         links.append(y)
-    return firsts, links, schurs, fits
+    return firsts, links, schurs
 
 def full_inverse(first, link, last):
     right = p3(link, last)
@@ -196,26 +201,25 @@
 
 
 def mega_kernel(
-    ph_hbm, ck_ref, pd_ref, w_ref, co_ref, sc_ref,
+    ph_hbm, ck_ref, pd_ref, w_ref, wt_ref, h_ref, total_ref, kn_ref, c1_ref,
     ph_ref, ph_sem, cg, sb, rb, bhi, blo_ref, ybuf, gs, gr, gg, zs, zr, zg, wq, wg, cp, cr, lhs,
     c_send, c_recv, y_send, y_recv, gs_send, gs_recv, gg_send, gg_recv,
     zs_send, zs_recv, zg_send, zg_recv, w_send, w_recv, f_send, f_recv,
 ):
     pair, tile = lax.axis_index("pair"), lax.axis_index("tile")
-    zh, zl, yl = pair // 4, (pair // 2) % 2, pair % 2
-    yh, xh, xl, core = tile // 8, (tile // 4) % 2, (tile // 2) % 2, tile % 2
+    zh, zl, yl = pair >> 2, (pair >> 1) & 1, pair & 1
+    yh, xh, xl, core = tile >> 3, (tile >> 2) & 1, (tile >> 1) & 1, tile & 1
     me = zl * 8 + yl * 4 + xl * 2 + core
     group = zh * 4 + yh * 2 + xh
 
     def place(a, r):
-        p = (a // 4) * 4 + (r // 8) * 2 + (r // 4) % 2
-        return p, ((a // 2) % 2) * 8 + (a % 2) * 4 + r % 4
+        return (a >> 2) * 4 + (r >> 2), ((a >> 1) & 1) * 8 + (a & 1) * 4 + (r & 3)
 
     def group_at(r, half):
         if half == 0:
             return group
         return (
-            ((zh + zl + r // 8) % 2) * 4 + ((yh + yl + (r // 4) % 2) % 2) * 2 + (xh + xl + (r // 2) % 2) % 2
+            ((zh + zl + (r >> 3)) & 1) * 4 + ((yh + yl + (r >> 2)) & 1) * 2 + ((xh + xl + (r >> 1)) & 1)
         )
 
     def residue_peer(i):
@@ -303,7 +307,7 @@
     at = incidence_rows(rows[0:2, :].astype(jnp.int32))
     at16 = at.astype(BF16)
     xt = design_rows(at16)
-    firsts, links, schurs, fits = normal_parts(at, at16, xt, w)
+    normals, evens, fits = normal_parts(at, at16, xt, w)
     pl.semaphore_wait(barrier, 2 * N_TILE + N_PAIR - 3)
 
     code = ck_ref[0:1, :] * 65536 + ck_ref[1:2, :]
@@ -336,6 +340,7 @@
     for half in range(2):
         pack(me, half, rb.at[half, me])
 
+    firsts, links, schurs = eliminate_even(normals, evens)
     lasts = newton_start(schurs + fits, [1.0, 1.0, 0.5, 0.5])
     lasts = newton_steps(schurs + fits, lasts, 8)
     last0, last1, f0, f1 = newton_end(schurs + fits, lasts)
@@ -406,7 +411,7 @@
 
     for half in range(2):
         unpack(me, half)
-        loop(1, N_TILE, lambda i, half=half: y_arrive(i, half))
+        loop(1, N_TILE, lambda i, half=half: y_arrive(N_TILE - i, half))
         zt = lax.fori_loop(0, N_PAIR, functools.partial(z_body, half=half), zero)
         zs[half] = zt.reshape(N_TILE, KNOTS, SCREEN)
         start_residue(zs_copy, half)
@@ -474,16 +479,11 @@
     total = jnp.concatenate(totals, axis=1)
     wait_residue(w_copy)
 
-    wt = wg[...].reshape(SCREEN, 2 * 128)
-    q0 = wt[:, 0:128]
-    q1 = p3(h, q0)
-    ehi, elo = split2(q1[:, 0:NB].T)
-    own_knots = bhi[group]
-    co_ref[...] = total - (nn(ehi, own_knots) + nn(elo, own_knots))
-    step = wt[:, 128:128 + NB + OWN] - (q0[:, 0:NB + OWN] - q1[:, 0:NB + OWN])
-    change = step[:, NB:] - p3t(step[:, 0:NB], c1_own)
-    s2 = q1[:, NB + OWN:NB + 2 * OWN] + p3(h, change)
-    sc_ref[...] = s2.T[0:38]
+    wt_ref[...] = wg[...].reshape(SCREEN, 2 * 128)
+    h_ref[...] = h
+    total_ref[...] = total
+    kn_ref[...] = bhi[group]
+    c1_ref[...] = c1_own
 
     def drain_residue(i):
         other = residue_peer(i)
@@ -506,17 +506,33 @@
     loop(1, N_PAIR, drain_class)
 
 
+def tail_kernel(wt_ref, h_ref, total_ref, kn_ref, c1_ref, co_ref, sc_ref):
+    wt, h = wt_ref[...], h_ref[...]
+    q0 = wt[:, 0:128]
+    q1 = p3(h, q0)
+    ehi, elo = split2(q1[:, 0:NB].T)
+    knots = kn_ref[...]
+    co_ref[...] = total_ref[...] - (nn(ehi, knots) + nn(elo, knots))
+    step = wt[:, 128:128 + NB + OWN] - (q0[:, 0:NB + OWN] - q1[:, 0:NB + OWN])
+    change = step[:, NB:] - p3t(step[:, 0:NB], c1_ref[...])
+    s2 = q1[:, NB + OWN:NB + 2 * OWN] + p3(h, change)
+    sc_ref[...] = s2.T[0:38]
+
+
 def local(phases, pair_dates, weights, coords):
     vmem = pl.BlockSpec(memory_space=pltpu.VMEM)
     shape = jax.ShapeDtypeStruct
     dma = pltpu.SemaphoreType.DMA
     tiles, pairs = dma((N_TILE,)), dma((N_PAIR,))
     twos, halves, parts = dma((2, N_PAIR)), dma((2, N_TILE)), dma((2, N_TILE, PARTS))
-    return pl.pallas_call(
+    parts_out = pl.pallas_call(
         mega_kernel,
-        out_shape=[shape((NB, PIX), F32), shape((38, SCREEN), F32)],
+        out_shape=[
+            shape((SCREEN, 2 * 128), F32), shape((SCREEN, SCREEN), F32), shape((NB, PIX), F32),
+            shape((SCREEN, PIX), BF16), shape((OWN, NB), F32),
+        ],
         in_specs=[pl.BlockSpec(memory_space=pl.ANY)] + [vmem] * 3,
-        out_specs=[vmem] * 2,
+        out_specs=[vmem] * 5,
         scratch_shapes=[
             pltpu.VMEM((PAIRS, NPIX), BF16),
             dma,
@@ -545,6 +561,14 @@
         ),
         name="mega",
     )(phases, coords, pair_dates.T, weights)
+    return pl.pallas_call(
+        tail_kernel,
+        out_shape=[shape((NB, PIX), F32), shape((38, SCREEN), F32)],
+        in_specs=[vmem] * 5,
+        out_specs=[vmem] * 2,
+        compiler_params=pltpu.CompilerParams(vmem_limit_bytes=VMEM_LIMIT),
+        name="tail",
+    )(*parts_out)
 
 
 def solution(mesh):

time: 74.7 us -> 70.1 us (0.938)
  local copies, waits for them, and re-layouts: 2.97 us -> 0 us
  Pallas kernels: 70.9 us -> 69.2 us
    unnamed x2 -> x0, local copies, waits for them, and re-layouts: 2.97 us -> none
    pallas_call x1 -> x2, Pallas kernels: 70.9 us -> 69.2 us  [the longest x1 66.2 us: local(): pl.pallas_call(mega_kernel, out_shape=[shape((SCREEN, 2 * 128), F32), sha...]
where the time goes in v5:
time: 70.1 us; the launch traced here: 69.9 us
  Pallas kernels  69.2 us (99%)
    pallas_call x1, Pallas kernels, local(): pl.pallas_call(mega_kernel, out_shape=[shape((SCREEN, 2 * 128), F32), sha...  66.2 us
    pallas_call x1, Pallas kernels, local(): pl.pallas_call(tail_kernel, out_shape=[shape((NB, PIX), F32), shape((38,...  3.06 us

profile of v5, /device:TPU:1, one launch (start us, length us, event | category | flops | bytes accessed | tf_op | source)
XLA Modules:
  0.0 69.9 jit_solution(14301166708215259455)
XLA Ops:
  0.6 66.2 %mega.1 = (f32[256,256]{1,0:T(8,128)}, f32[256,256]{1,0:T(8,128)}, f32[32,1024]{1,0:T(8,128)}, bf16[256,1024]{1,0:T(8,128)(2,1)}, f32[40,32]{1,0:T(8,128)}) custom-call(bf16[12,131072]{1,0:T(8,128)(2,1)} %ph_hbm.1, s32[2,1024]{1,0:T(2,128)} %ck_ref.1, s32[2,1536]{1,0:T(2,128)} %bitcast.1, f32[2,1536]{1,0:T(2,128)} %w_ref.1), custom_call_target="tpu_custom_call" | custom-call | tf_op jit(solution)/shard_map/mega/pallas_call | solution.py:528
  66.8 3.1 %tail.1 = (f32[32,1024]{1,0:T(8,128)}, f32[38,256]{1,0:T(8,128)}) custom-call(f32[256,256]{1,0:T(8,128)} %get-tuple-element.7.wt_ref, f32[256,256]{1,0:T(8,128)} %get-tuple-element.8.h_ref, f32[32,1024]{1,0:T(8,128)} %get-tuple-element.9.total_ref, bf16[256,1024]{1,0:T(8,128)(2,1)} %get-tuple-element.10.kn_ref, f32[40,32]{1,0:T(8,128)} %get-tuple-element.11.c1_ref), custom_call_target="tpu_custom_call" | custom-call | tf_op jit(solution)/shard_map/tail/pallas_call | solution.py:564

commit v6 on v5

--- a/solution.py
+++ b/solution.py
@@ -230,6 +230,16 @@
         t = group + i
         return jnp.where(t >= N_PAIR, t - N_PAIR, t)
 
+    def residue_far(i):
+        k = N_TILE - i
+        return (
+            ((zl + (k >> 3)) & 1) * 8 + ((yl + (k >> 2)) & 1) * 4 + ((xl + (k >> 1)) & 1) * 2 + ((core + k) & 1)
+        )
+
+    def class_far(i):
+        k = N_PAIR - i
+        return ((zh + (k >> 2)) & 1) * 4 + ((yh + (k >> 1)) & 1) * 2 + ((xh + k) & 1)
+
     def loop(lo, hi, f):
         def body(i, carry):
             f(i)
@@ -279,13 +289,19 @@
         return to_class(cp.at[half, other], cr.at[half], f_send.at[half], f_recv.at[half], other, slot)
 
     def start_residue(copy, *more):
-        loop(1, N_TILE, lambda i: copy(residue_peer(i), me, *more).start())
+        loop(1, N_TILE, lambda i: copy(residue_far(i), me, *more).start())
 
     def wait_residue(copy, *more):
         loop(1, N_TILE, lambda i: copy(residue_peer(i), residue_peer(i), *more).wait_recv())
 
+    def sent_residue(copy, *more):
+        loop(1, N_TILE, lambda i: copy(residue_peer(i), me, *more).wait_send())
+
+    def sent_class(copy, *more):
+        loop(1, N_PAIR, lambda i: copy(class_peer(i), group, *more).wait_send())
+
     def start_class(copy, *more):
-        loop(1, N_PAIR, lambda i: copy(class_peer(i), group, *more).start())
+        loop(1, N_PAIR, lambda i: copy(class_far(i), group, *more).start())
 
     def wait_class(copy, *more):
         loop(1, N_PAIR, lambda i: copy(class_peer(i), class_peer(i), *more).wait_recv())
@@ -297,17 +313,10 @@
     def greet(where):
         pl.semaphore_signal(barrier, inc=1, device_id=where, device_id_type=MESH)
 
-    for half in range(2):
-        loop(1, N_TILE, lambda i, half=half: greet(place(group_at(residue_peer(i), half), residue_peer(i))))
-    loop(1, N_PAIR, lambda i: greet(place(class_peer(i), me)))
-
-    rows = jnp.concatenate([pd_ref[...].astype(F32), w_ref[...], jnp.zeros((4, KP), F32)], axis=0)
-    rows = by_group(rows)
-    w = rows[2:4, :]
-    at = incidence_rows(rows[0:2, :].astype(jnp.int32))
-    at16 = at.astype(BF16)
-    xt = design_rows(at16)
-    normals, evens, fits = normal_parts(at, at16, xt, w)
+    loop(1, N_PAIR, lambda i: greet(place(class_far(i), me)))
+    for half in range(2):
+        loop(1, N_TILE, lambda i, half=half: greet(place(group_at(residue_far(i), half), residue_far(i))))
+
     pl.semaphore_wait(barrier, 2 * N_TILE + N_PAIR - 3)
 
     code = ck_ref[0:1, :] * 65536 + ck_ref[1:2, :]
@@ -340,31 +349,17 @@
     for half in range(2):
         pack(me, half, rb.at[half, me])
 
+    rows = jnp.concatenate([pd_ref[...].astype(F32), w_ref[...], jnp.zeros((4, KP), F32)], axis=0)
+    rows = by_group(rows)
+    w = rows[2:4, :]
+    at = incidence_rows(rows[0:2, :].astype(jnp.int32))
+    at16 = at.astype(BF16)
+    xt = design_rows(at16)
+    normals, evens, fits = normal_parts(at, at16, xt, w)
     firsts, links, schurs = eliminate_even(normals, evens)
     lasts = newton_start(schurs + fits, [1.0, 1.0, 0.5, 0.5])
     lasts = newton_steps(schurs + fits, lasts, 8)
     last0, last1, f0, f1 = newton_end(schurs + fits, lasts)
-
-    wait_class(c_copy)
-    centers = iota((KNOTS, 1), 0).astype(F32) - 1.0
-
-    def knots(p, carry):
-        g1, g2 = carry
-        for i in range(PIX // 128):
-            rows, cols = knot_rows(cg[p, i:i + 1, :], centers)
-            lanes = pl.ds(i * 128, 128)
-            for m in range(KNOTS):
-                hi, lo = split2(rows[m:m + 1, :] * cols)
-                bhi[p, m * KNOTS:(m + 1) * KNOTS, lanes] = hi
-                blo_ref[m * KNOTS:(m + 1) * KNOTS, lanes] = lo
-        hi = bhi[p]
-        return g1 + nt(hi, hi), g2 + nt(hi, blo_ref[...])
-
-    zero = jnp.zeros((SCREEN, SCREEN), F32)
-    g1, g2 = lax.fori_loop(0, N_PAIR, knots, (zero, zero))
-    gs[...] = (g1 + g2 + g2.T).reshape(N_TILE, KNOTS, SCREEN)
-    start_residue(gs_copy)
-    gr[me] = gs[me]
 
     sel = near_dates(zh)
     fit0 = (p3(f0, xt) * w[0:1, :]).astype(BF16)
@@ -381,12 +376,27 @@
     ends = jnp.concatenate([nt(fit1, at16), nt(d1, at16), sel], axis=0)
     fit_own = [nn(fit1, spread_own(functools.partial(group_at, half=half))).astype(BF16) for half in range(2)]
 
-    wait_residue(gs_copy)
-    gsum = gr[0]
-    for t in range(1, N_TILE):
-        gsum = gsum + gr[t]
-    gg[me] = gsum
-    start_residue(gg_copy)
+    wait_class(c_copy)
+    centers = iota((KNOTS, 1), 0).astype(F32) - 1.0
+
+    def knots(p, carry):
+        g1, g2 = carry
+        for i in range(PIX // 128):
+            rows, cols = knot_rows(cg[p, i:i + 1, :], centers)
+            lanes = pl.ds(i * 128, 128)
+            for m in range(KNOTS):
+                hi, lo = split2(rows[m:m + 1, :] * cols)
+                bhi[p, m * KNOTS:(m + 1) * KNOTS, lanes] = hi
+                blo_ref[m * KNOTS:(m + 1) * KNOTS, lanes] = lo
+        hi = bhi[p]
+        return g1 + nt(hi, hi), g2 + nt(hi, blo_ref[...])
+
+    zero = jnp.zeros((SCREEN, SCREEN), F32)
+    g1, g2 = lax.fori_loop(0, N_PAIR, knots, (zero, zero))
+    gs[...] = (g1 + g2 + g2.T).reshape(N_TILE, KNOTS, SCREEN)
+    start_residue(gs_copy)
+    gr[me] = gs[me]
+
 
     def unpack(t, half):
         rest = [rb[half, t, 4 + a].astype(F32) for a in range(2)]
@@ -417,11 +427,18 @@
         start_residue(zs_copy, half)
         zr[half, me] = zs[half, me]
         cr[half, group] = cp[half, group]
-    wait_residue(gg_copy)
-    gram = gg[...].reshape(SCREEN, SCREEN)
-    gram = gram + jnp.where(iota((SCREEN, SCREEN), 0) == iota((SCREEN, SCREEN), 1), 1.0, 0.0)
-    state = newton_start([gram], [1.0])
-    state = newton_steps([gram], state, 3)
+    sent_class(c_copy)
+    sent_residue(gs_copy)
+    for half in range(2):
+        for part in range(PARTS):
+            sent_residue(y_copy, half, part)
+    wait_residue(gs_copy)
+    gsum = gr[0]
+    for t in range(1, N_TILE):
+        gsum = gsum + gr[t]
+    gg[me] = gsum
+    start_residue(gg_copy)
+
     sums = []
     for half in range(2):
         wait_residue(zs_copy, half)
@@ -433,7 +450,14 @@
     start_class(zg_copy)
     for half in range(2):
         start_class(f_copy, half)
-    state = newton_steps([gram], state, 3)
+    wait_residue(gg_copy)
+    gram = gg[...].reshape(SCREEN, SCREEN)
+    gram = gram + jnp.where(iota((SCREEN, SCREEN), 0) == iota((SCREEN, SCREEN), 1), 1.0, 0.0)
+    state = newton_start([gram], [1.0])
+    state = newton_steps([gram], state, 5)
+    sent_residue(gg_copy)
+    for half in range(2):
+        sent_residue(zs_copy, half)
     wait_class(zg_copy)
     octant = iota((1, SCREEN), 1)
     octant = jnp.where(octant < GROUP, (octant * 10923) >> 18, -1)
@@ -463,8 +487,9 @@
         ], axis=1)
     start_residue(w_copy)
     wg[me] = wq[me // 4]
-    state = newton_steps([gram], state, 3)
+    state = newton_steps([gram], state, 4)
     (h,) = newton_end([gram], state)
+    sent_class(zg_copy)
     mine = zl * 2 + yl
     c1_own = c1[0:OWN]
     for n in range(1, 4):
@@ -485,25 +510,9 @@
     kn_ref[...] = bhi[group]
     c1_ref[...] = c1_own
 
-    def drain_residue(i):
-        other = residue_peer(i)
-        for half in range(2):
-            for part in range(PARTS):
-                y_copy(other, me, half, part).wait_send()
-            zs_copy(other, me, half).wait_send()
-        for copy in (gs_copy, gg_copy, w_copy):
-            copy(other, me).wait_send()
-
-    loop(1, N_TILE, drain_residue)
-
-    def drain_class(i):
-        other = class_peer(i)
-        for copy in (c_copy, zg_copy):
-            copy(other, group).wait_send()
-        for half in range(2):
-            f_copy(other, group, half).wait_send()
-
-    loop(1, N_PAIR, drain_class)
+    sent_residue(w_copy)
+    for half in range(2):
+        sent_class(f_copy, half)
 
 
 def tail_kernel(wt_ref, h_ref, total_ref, kn_ref, c1_ref, co_ref, sc_ref):

time: 70.1 us -> 67.1 us (0.957)
  Pallas kernels: 69.2 us -> 66.3 us
    pallas_call x1, Pallas kernels: 66.2 us -> 63.2 us  [local(): pl.pallas_call(mega_kernel, out_shape=[shape((SCREEN, 2 * 128), F32), sha...]
where the time goes in v6:
time: 67.1 us; the launch traced here: 66.9 us
  Pallas kernels  66.3 us (99%)
    pallas_call x1, Pallas kernels, local(): pl.pallas_call(mega_kernel, out_shape=[shape((SCREEN, 2 * 128), F32), sha...  63.2 us
    pallas_call x1, Pallas kernels, local(): pl.pallas_call(tail_kernel, out_shape=[shape((NB, PIX), F32), shape((38,...  3.06 us

profile of v6, /device:TPU:1, one launch (start us, length us, event | category | flops | bytes accessed | tf_op | source)
XLA Modules:
  0.0 66.9 jit_solution(195308511961481450)
XLA Ops:
  0.6 63.2 %mega.1 = (f32[256,256]{1,0:T(8,128)}, f32[256,256]{1,0:T(8,128)}, f32[32,1024]{1,0:T(8,128)}, bf16[256,1024]{1,0:T(8,128)(2,1)}, f32[40,32]{1,0:T(8,128)}) custom-call(bf16[12,131072]{1,0:T(8,128)(2,1)} %ph_hbm.1, s32[2,1024]{1,0:T(2,128)} %ck_ref.1, s32[2,1536]{1,0:T(2,128)} %bitcast.1, f32[2,1536]{1,0:T(2,128)} %w_ref.1), custom_call_target="tpu_custom_call" | custom-call | tf_op jit(solution)/shard_map/mega/pallas_call | solution.py:537
  63.8 3.1 %tail.1 = (f32[32,1024]{1,0:T(8,128)}, f32[38,256]{1,0:T(8,128)}) custom-call(f32[256,256]{1,0:T(8,128)} %get-tuple-element.7.wt_ref, f32[256,256]{1,0:T(8,128)} %get-tuple-element.8.h_ref, f32[32,1024]{1,0:T(8,128)} %get-tuple-element.9.total_ref, bf16[256,1024]{1,0:T(8,128)(2,1)} %get-tuple-element.10.kn_ref, f32[40,32]{1,0:T(8,128)} %get-tuple-element.11.c1_ref), custom_call_target="tpu_custom_call" | custom-call | tf_op jit(solution)/shard_map/tail/pallas_call | solution.py:573

commit v7 on v6

--- a/solution.py
+++ b/solution.py
@@ -364,16 +364,6 @@
     sel = near_dates(zh)
     fit0 = (p3(f0, xt) * w[0:1, :]).astype(BF16)
     fit1 = (p3(f1, xt) * w[1:2, :]).astype(BF16)
-    d0 = date_solve(full_inverse(firsts[0], links[0], last0), at16, w[0:1, :])
-    d1 = date_solve(p3(sel, full_inverse(firsts[1], links[1], last1)), at16, w[1:2, :])
-    lhs[0:DATES] = d0
-    lhs[DATES:F0_AT] = jnp.zeros((F0_AT - DATES, KP), BF16)
-    lhs[F0_AT:D1_AT] = jnp.concatenate([fit0, fit1], axis=0)
-    lhs[D1_AT:ROWS] = d1
-    xhi, xlo = split2(xt)
-    c0 = nt(d0, xhi) + nt(d0, xlo)
-    c1 = nt(d1, xhi) + nt(d1, xlo)
-    ends = jnp.concatenate([nt(fit1, at16), nt(d1, at16), sel], axis=0)
     fit_own = [nn(fit1, spread_own(functools.partial(group_at, half=half))).astype(BF16) for half in range(2)]
 
     wait_class(c_copy)
@@ -439,6 +429,13 @@
     gg[me] = gsum
     start_residue(gg_copy)
 
+    d0 = date_solve(full_inverse(firsts[0], links[0], last0), at16, w[0:1, :])
+    d1 = date_solve(p3(sel, full_inverse(firsts[1], links[1], last1)), at16, w[1:2, :])
+    lhs[0:DATES] = d0
+    lhs[DATES:F0_AT] = jnp.zeros((F0_AT - DATES, KP), BF16)
+    lhs[F0_AT:D1_AT] = jnp.concatenate([fit0, fit1], axis=0)
+    lhs[D1_AT:ROWS] = d1
+
     sums = []
     for half in range(2):
         wait_residue(zs_copy, half)
@@ -450,6 +447,10 @@
     start_class(zg_copy)
     for half in range(2):
         start_class(f_copy, half)
+    xhi, xlo = split2(xt)
+    c0 = nt(d0, xhi) + nt(d0, xlo)
+    c1 = nt(d1, xhi) + nt(d1, xlo)
+    ends = jnp.concatenate([nt(fit1, at16), nt(d1, at16), sel], axis=0)
     wait_residue(gg_copy)
     gram = gg[...].reshape(SCREEN, SCREEN)
     gram = gram + jnp.where(iota((SCREEN, SCREEN), 0) == iota((SCREEN, SCREEN), 1), 1.0, 0.0)

time: 67.1 us -> 64.9 us (0.967)
  Pallas kernels: 66.3 us -> 64 us
    pallas_call x1, Pallas kernels: 63.2 us -> 61 us  [local(): pl.pallas_call(mega_kernel, out_shape=[shape((SCREEN, 2 * 128), F32), sha...]
where the time goes in v7:
time: 64.9 us; the launch traced here: 64.7 us
  Pallas kernels  64 us (99%)
    pallas_call x1, Pallas kernels, local(): pl.pallas_call(mega_kernel, out_shape=[shape((SCREEN, 2 * 128), F32), sha...  61 us
    pallas_call x1, Pallas kernels, local(): pl.pallas_call(tail_kernel, out_shape=[shape((NB, PIX), F32), shape((38,...  3.06 us

profile of v7, /device:TPU:1, one launch (start us, length us, event | category | flops | bytes accessed | tf_op | source)
XLA Modules:
  0.0 64.7 jit_solution(14051149228563552858)
XLA Ops:
  0.6 61.0 %mega.1 = (f32[256,256]{1,0:T(8,128)}, f32[256,256]{1,0:T(8,128)}, f32[32,1024]{1,0:T(8,128)}, bf16[256,1024]{1,0:T(8,128)(2,1)}, f32[40,32]{1,0:T(8,128)}) custom-call(bf16[12,131072]{1,0:T(8,128)(2,1)} %ph_hbm.1, s32[2,1024]{1,0:T(2,128)} %ck_ref.1, s32[2,1536]{1,0:T(2,128)} %bitcast.1, f32[2,1536]{1,0:T(2,128)} %w_ref.1), custom_call_target="tpu_custom_call" | custom-call | tf_op jit(solution)/shard_map/mega/pallas_call | solution.py:538
  61.6 3.1 %tail.1 = (f32[32,1024]{1,0:T(8,128)}, f32[38,256]{1,0:T(8,128)}) custom-call(f32[256,256]{1,0:T(8,128)} %get-tuple-element.7.wt_ref, f32[256,256]{1,0:T(8,128)} %get-tuple-element.8.h_ref, f32[32,1024]{1,0:T(8,128)} %get-tuple-element.9.total_ref, bf16[256,1024]{1,0:T(8,128)(2,1)} %get-tuple-element.10.kn_ref, f32[40,32]{1,0:T(8,128)} %get-tuple-element.11.c1_ref), custom_call_target="tpu_custom_call" | custom-call | tf_op jit(solution)/shard_map/tail/pallas_call | solution.py:574

commit v8 on v7

--- a/solution.py
+++ b/solution.py
@@ -406,7 +406,6 @@
 
     def z_body(p, acc, half):
         y = ybuf[half, p]
-        cp[half, p] = nn(fit_own[half], y).astype(BF16)
         return acc + nt(bhi[p, :, half * HALF:(half + 1) * HALF], y)
 
     for half in range(2):
@@ -416,7 +415,6 @@
         zs[half] = zt.reshape(N_TILE, KNOTS, SCREEN)
         start_residue(zs_copy, half)
         zr[half, me] = zs[half, me]
-        cr[half, group] = cp[half, group]
     sent_class(c_copy)
     sent_residue(gs_copy)
     for half in range(2):
@@ -446,7 +444,12 @@
     zg[group] = nn(jnp.concatenate(sums, axis=0), squeeze()).astype(BF16)
     start_class(zg_copy)
     for half in range(2):
+        def fit_body(p, half=half):
+            cp[half, p] = nn(fit_own[half], ybuf[half, p]).astype(BF16)
+
+        loop(0, N_PAIR, fit_body)
         start_class(f_copy, half)
+        cr[half, group] = cp[half, group]
     xhi, xlo = split2(xt)
     c0 = nt(d0, xhi) + nt(d0, xlo)
     c1 = nt(d1, xhi) + nt(d1, xlo)

time: 64.9 us -> 64.9 us (level)
  no operation moved by 1% of the time
where the time goes in v8:
time: 64.9 us; the launch traced here: 64.7 us
  Pallas kernels  64.1 us (99%)
    pallas_call x1, Pallas kernels, local(): pl.pallas_call(mega_kernel, out_shape=[shape((SCREEN, 2 * 128), F32), sha...  61 us
    pallas_call x1, Pallas kernels, local(): pl.pallas_call(tail_kernel, out_shape=[shape((NB, PIX), F32), shape((38,...  3.06 us

profile of v8, /device:TPU:1, one launch (start us, length us, event | category | flops | bytes accessed | tf_op | source)
XLA Modules:
  0.0 64.7 jit_solution(4679072815884849793)
XLA Ops:
  0.6 61.0 %mega.1 = (f32[256,256]{1,0:T(8,128)}, f32[256,256]{1,0:T(8,128)}, f32[32,1024]{1,0:T(8,128)}, bf16[256,1024]{1,0:T(8,128)(2,1)}, f32[40,32]{1,0:T(8,128)}) custom-call(bf16[12,131072]{1,0:T(8,128)(2,1)} %ph_hbm.1, s32[2,1024]{1,0:T(2,128)} %ck_ref.1, s32[2,1536]{1,0:T(2,128)} %bitcast.1, f32[2,1536]{1,0:T(2,128)} %w_ref.1), custom_call_target="tpu_custom_call" | custom-call | tf_op jit(solution)/shard_map/mega/pallas_call | solution.py:541
  61.7 3.1 %tail.1 = (f32[32,1024]{1,0:T(8,128)}, f32[38,256]{1,0:T(8,128)}) custom-call(f32[256,256]{1,0:T(8,128)} %get-tuple-element.7.wt_ref, f32[256,256]{1,0:T(8,128)} %get-tuple-element.8.h_ref, f32[32,1024]{1,0:T(8,128)} %get-tuple-element.9.total_ref, bf16[256,1024]{1,0:T(8,128)(2,1)} %get-tuple-element.10.kn_ref, f32[40,32]{1,0:T(8,128)} %get-tuple-element.11.c1_ref), custom_call_target="tpu_custom_call" | custom-call | tf_op jit(solution)/shard_map/tail/pallas_call | solution.py:577
